TPU v7x, 32 devices: a whole 2x2x4 slice. The times are simulated.
32 devices in a mesh: seq: 8 (over z, x), head: 4 (over y, core).
Axes of the slice: x: 2, y: 2, z: 4, core: 2. Of those that a mesh axis runs over, the one named last changes fastest.
Arguments:
- block_input: bfloat16 [1, 1024, 1024], P(None, 'seq', 'head'), may hold values from -6 to 6
- norm_gain: float32 [1024], replicated, may hold values from 0.5 to 1.5
- w_query: bfloat16 [1024, 512], P(None, 'head'), may hold values from -0.1875 to 0.1875
- w_key: bfloat16 [1024, 512], P(None, 'head'), may hold values from -0.1875 to 0.1875
- w_value: bfloat16 [1024, 1024], P(None, 'head'), may hold values from -0.1875 to 0.1875
- w_outgate: bfloat16 [1024, 1024], P(None, 'head'), may hold values from -0.1875 to 0.1875
- w_rank: bfloat16 [1024, 16], replicated, may hold values from -0.1875 to 0.1875
- w_expand: bfloat16 [16, 512], P(None, 'head'), may hold values from -1.5 to 1.5
- gate_bias: float32 [512], P('head'), may hold values from 0.3 to 10, as said below
- w_output: bfloat16 [1024, 1024], P('head'), may hold values from -0.1875 to 0.1875
- ffn_gain: float32 [1024], replicated, may hold values from 0.5 to 1.5
- w_gate: bfloat16 [1024, 2816], P(None, 'head'), may hold values from -0.1875 to 0.1875
- w_up: bfloat16 [1024, 2816], P(None, 'head'), may hold values from -0.1875 to 0.1875
- w_down: bfloat16 [2816, 1024], P('head'), may hold values from -0.109375 to 0.109375
- cotangent: bfloat16 [1, 1024, 1024], P(None, 'seq', 'head'), may hold values from -6 to 6
Outputs:
- output: bfloat16 [1, 1024, 1024], P(None, 'seq', 'head')
- grad_input: float32 [1, 1024, 1024], P(None, 'seq', 'head')
- grad_norm_gain: float32 [1024], P('head')
- grad_w_query: float32 [1024, 512], P('seq', 'head')
- grad_w_key: float32 [1024, 512], P('seq', 'head')
- grad_w_value: float32 [1024, 1024], P('seq', 'head')
- grad_w_outgate: float32 [1024, 1024], P('seq', 'head')
- grad_w_rank: float32 [1024, 16], P('seq')
- grad_w_expand: float32 [16, 512], P(None, 'head')
- grad_gate_bias: float32 [512], P('head')
- grad_w_output: float32 [1024, 1024], P('head', 'seq')
- grad_ffn_gain: float32 [1024], P('head')
- grad_w_gate: float32 [1024, 2816], P('seq', 'head')
- grad_w_up: float32 [1024, 2816], P('seq', 'head')
- grad_w_down: float32 [2816, 1024], P('head', 'seq')
Inputs may be any that keep to these rules, and one draw needn't show every extreme that they name: `gate_bias`: bias of the forget gate's logits.
All inputs are finite; a program needn't handle non-finite values.
Results may differ from a plain program's by a relative error of at most 0.012.
Values may be sent and summed in bfloat16 or wider, within the bound.
A program may use at most 128 MiB of HBM per device.

v0:
```python
import jax
import jax.numpy as jnp
from jax import lax
from jax.sharding import PartitionSpec as P

GROUP = 64


EPS = 1e-06
HEAD_EPS = 1e-05
PRECISE = lax.Precision.HIGHEST


def carried_in(shard, axis, combine, identity, reverse):
    peers, here = (lax.axis_size(axis), lax.axis_index(axis))
    everything = jax.tree.map(lambda part: lax.all_gather(part, axis), shard)
    start = jax.tree.map(
        lambda part, zero: jnp.broadcast_to(jnp.asarray(zero, part.dtype), part.shape),
        shard,
        identity,
    )

    def turn(k, before):
        at = peers - 1 - k if reverse else k
        reached = at > here if reverse else at < here
        new = combine(before, jax.tree.map(lambda part: part[at], everything))
        return jax.tree.map(lambda a, b: jnp.where(reached, a, b), new, before)

    return lax.fori_loop(0, peers, turn, start)


def matmul_high(left_side, right_side):
    return jnp.dot(left_side, right_side, precision=PRECISE)


def rows_product(left_side, right_side):
    return lax.dot_general(
        left_side, right_side, (((0,), (0,)), ((), ())), preferred_element_type=jnp.float32
    )


def cross_product(left_side, right_side):
    return lax.dot_general(
        left_side, right_side, (((1,), (1,)), ((), ())), preferred_element_type=jnp.float32
    )


def group_step(carry_state, block_inputs):
    q_block, k_block, v_block, g_block = block_inputs
    block_len = q_block.shape[0]
    cumulative = jnp.cumsum(g_block, axis=0)
    final_sum = cumulative[-1]
    q_decay = q_block * jnp.exp(cumulative)
    k_decay = k_block * jnp.exp(-cumulative)
    scores = matmul_high(q_decay, k_decay.T)
    row_index = lax.broadcasted_iota(jnp.int32, (block_len, block_len), 0)
    col_index = lax.broadcasted_iota(jnp.int32, (block_len, block_len), 1)
    scores = jnp.where(row_index >= col_index, scores, jnp.zeros_like(scores))
    block_out = matmul_high(q_decay, carry_state) + matmul_high(scores, v_block)
    k_tail = k_block * jnp.exp(final_sum - cumulative)
    carry_state = jnp.exp(final_sum)[:, None] * carry_state + matmul_high(k_tail.T, v_block)
    return (carry_state, block_out)


def span_run(q_seq, k_seq, v_seq, g_seq, start_state):
    blocks = q_seq.shape[0] // GROUP

    def to_blocks(tensor):
        return tensor.reshape(blocks, GROUP, tensor.shape[-1])

    end_state, block_outs = lax.scan(
        jax.checkpoint(group_step),
        start_state,
        (to_blocks(q_seq), to_blocks(k_seq), to_blocks(v_seq), to_blocks(g_seq)),
    )
    return (block_outs.reshape(q_seq.shape[0], v_seq.shape[-1]), end_state)


def run_all(q_all, k_all, v_all, g_all, start_all):
    return jax.vmap(span_run)(q_all, k_all, v_all, g_all, start_all)


def combine(earlier, later):
    return (earlier[0] + later[0], jnp.exp(later[0])[:, :, None] * earlier[1] + later[1])


def body(
    block_input,
    norm_gain,
    w_query,
    w_key,
    w_value,
    w_outgate,
    w_rank,
    w_expand,
    gate_bias,
    w_output,
    ffn_gain,
    w_gate,
    w_up,
    w_down,
    cotangent,
):
    seq_count, span_len, part_width = block_input.shape
    row_count = seq_count * span_len
    head_count = lax.axis_size("head")
    full_width = part_width * head_count
    col_start = lax.axis_index("head") * part_width
    key_width = w_query.shape[1]
    value_width = w_value.shape[1]
    query_scale = key_width ** (-0.5)

    def per_seq(tensor):
        return tensor.reshape(seq_count, span_len, tensor.shape[-1])

    def mine(tensor):
        return lax.dynamic_slice_in_dim(tensor, col_start, part_width, tensor.ndim - 1)

    input_part = block_input.reshape(row_count, part_width)
    input_rows = lax.all_gather(input_part, "head", axis=1, tiled=True)
    input_wide = input_rows.astype(jnp.float32)
    inverse_one = lax.rsqrt(jnp.mean(input_wide * input_wide, axis=1, keepdims=True) + EPS)
    normal_one = input_wide * inverse_one
    normed = (normal_one * norm_gain).astype(jnp.bfloat16)
    query_proj = jnp.dot(normed, w_query, preferred_element_type=jnp.float32)
    key_proj = jnp.dot(normed, w_key, preferred_element_type=jnp.float32)
    value_proj = jnp.dot(normed, w_value, preferred_element_type=jnp.float32)
    outgate = jnp.dot(normed, w_outgate, preferred_element_type=jnp.float32)
    lowrank = jnp.dot(normed, w_rank, preferred_element_type=jnp.float32)
    expand_wide = w_expand.astype(jnp.float32)
    preact = matmul_high(lowrank, expand_wide) + gate_bias
    logdecay = jax.nn.log_sigmoid(preact) / 16.0
    q_seq = per_seq(query_proj) * query_scale
    k_seq = per_seq(key_proj)
    v_seq = per_seq(value_proj)
    g_seq = per_seq(logdecay)
    zero_state = jnp.zeros((seq_count, key_width, value_width), jnp.float32)
    local_out, local_state = run_all(q_seq, k_seq, v_seq, g_seq, zero_state)
    cumulative = jnp.cumsum(g_seq, axis=1)
    carry_query = q_seq * jnp.exp(cumulative)
    decay_total = cumulative[:, -1, :]
    identity = (jnp.zeros_like(decay_total), zero_state)
    scanned = carried_in((decay_total, local_state), "seq", combine, identity, False)
    entering = scanned[1]
    mixer_out = local_out + jnp.einsum("sti,siv->stv", carry_query, entering, precision=PRECISE)
    mixer_out = mixer_out.reshape(row_count, value_width)
    head_inv = lax.rsqrt(jnp.mean(mixer_out * mixer_out, axis=1, keepdims=True) + HEAD_EPS)
    head_norm = mixer_out * head_inv
    outgate_sig = jax.nn.sigmoid(outgate)
    swish_gate = outgate * outgate_sig
    branch = (head_norm * swish_gate).astype(jnp.bfloat16)
    attn_part = jnp.dot(branch, w_output, preferred_element_type=jnp.float32)
    attn_mine = lax.psum_scatter(attn_part, "head", scatter_dimension=1, tiled=True)
    middle_part = input_part.astype(jnp.float32) + attn_mine
    middle_low = lax.all_gather(middle_part.astype(jnp.bfloat16), "head", axis=1, tiled=True)
    middle_wide = middle_low.astype(jnp.float32)
    inverse_two = lax.rsqrt(jnp.mean(middle_wide * middle_wide, axis=1, keepdims=True) + EPS)
    normal_two = middle_wide * inverse_two
    normed_two = (normal_two * ffn_gain).astype(jnp.bfloat16)
    gate_pre = jnp.dot(normed_two, w_gate, preferred_element_type=jnp.float32)
    up_pre = jnp.dot(normed_two, w_up, preferred_element_type=jnp.float32)
    gate_sig = jax.nn.sigmoid(gate_pre)
    hidden = (gate_pre * gate_sig * up_pre).astype(jnp.bfloat16)
    ffn_part = jnp.dot(hidden, w_down, preferred_element_type=jnp.float32)
    ffn_mine = lax.psum_scatter(
        ffn_part.astype(jnp.bfloat16), "head", scatter_dimension=1, tiled=True
    ).astype(jnp.float32)
    output = (middle_part + ffn_mine).astype(jnp.bfloat16).reshape(seq_count, span_len, part_width)
    grad_part = cotangent.reshape(row_count, part_width)
    grad_rows = lax.all_gather(grad_part, "head", axis=1, tiled=True)
    grad_wdown = rows_product(hidden, grad_rows)
    grad_hidden = cross_product(grad_rows, w_down)
    grad_gate = (grad_hidden * up_pre * gate_sig * (1.0 + gate_pre * (1.0 - gate_sig))).astype(
        jnp.bfloat16
    )
    grad_upper = (grad_hidden * gate_pre * gate_sig).astype(jnp.bfloat16)
    grad_wgate = rows_product(normed_two, grad_gate)
    grad_wup = rows_product(normed_two, grad_upper)
    grad_normed_two = cross_product(grad_gate, w_gate) + cross_product(grad_upper, w_up)
    stat_part = jnp.sum(grad_normed_two * ffn_gain * normal_two, axis=1, keepdims=True)
    grad_two, stat_two = (
        lax.psum_scatter(grad_normed_two, "head", scatter_dimension=1, tiled=True),
        lax.psum_scatter(
            jnp.tile(stat_part, (1, head_count)), "head", scatter_dimension=1, tiled=True
        ),
    )
    normal_mine = mine(normal_two)
    grad_middle = grad_part.astype(jnp.float32) + inverse_two * (
        grad_two * mine(ffn_gain) - normal_mine * stat_two / full_width
    )
    gain_two = jnp.sum(grad_two * normal_mine, axis=0)
    grad_branch_rows = lax.all_gather(grad_middle.astype(jnp.bfloat16), "head", axis=1, tiled=True)
    grad_wout = rows_product(branch, grad_branch_rows)
    grad_branch = cross_product(grad_branch_rows, w_output)
    grad_head = grad_branch * swish_gate
    grad_outgate = (
        grad_branch * head_norm * outgate_sig * (1.0 + outgate * (1.0 - outgate_sig))
    ).astype(jnp.bfloat16)
    grad_mixed = head_inv * (
        grad_head - head_norm * jnp.mean(grad_head * head_norm, axis=1, keepdims=True)
    )
    grad_seq = per_seq(grad_mixed)
    state_pull = jnp.einsum("sti,stv->siv", carry_query, grad_seq, precision=PRECISE)
    later = carried_in((decay_total, state_pull), "seq", combine, identity, True)
    later_grad = later[1]
    _, back_fn = jax.vjp(run_all, q_seq, k_seq, v_seq, g_seq, entering)
    grad_qseq, grad_kseq, grad_vseq, grad_gseq, _ = back_fn((grad_seq, later_grad))
    grad_query = (grad_qseq.reshape(row_count, key_width) * query_scale).astype(jnp.bfloat16)
    grad_keys = grad_kseq.reshape(row_count, key_width).astype(jnp.bfloat16)
    grad_values = grad_vseq.reshape(row_count, value_width).astype(jnp.bfloat16)
    grad_pre = grad_gseq.reshape(row_count, key_width) / 16.0 * jax.nn.sigmoid(-preact)
    grad_expand = lax.dot_general(lowrank, grad_pre, (((0,), (0,)), ((), ())), precision=PRECISE)
    grad_bias = jnp.sum(grad_pre, axis=0)
    grad_lowrank = lax.dot_general(
        grad_pre, expand_wide, (((1,), (1,)), ((), ())), precision=PRECISE
    )
    rank_wide = w_rank.astype(jnp.float32)
    grad_normed = (
        cross_product(grad_query, w_query)
        + cross_product(grad_keys, w_key)
        + cross_product(grad_values, w_value)
        + cross_product(grad_outgate, w_outgate)
        + lax.dot_general(grad_lowrank, rank_wide, (((1,), (1,)), ((), ())), precision=PRECISE)
    )
    stat_one_part = jnp.sum(grad_normed * norm_gain * normal_one, axis=1, keepdims=True)
    grad_one, stat_one, lowrank_total = (
        lax.psum_scatter(
            grad_normed.astype(jnp.bfloat16), "head", scatter_dimension=1, tiled=True
        ).astype(jnp.float32),
        lax.psum_scatter(
            jnp.tile(stat_one_part, (1, head_count)).astype(jnp.bfloat16),
            "head",
            scatter_dimension=1,
            tiled=True,
        ).astype(jnp.float32),
        lax.psum_scatter(
            jnp.tile(grad_lowrank, (1, head_count)).astype(jnp.bfloat16),
            "head",
            scatter_dimension=1,
            tiled=True,
        ).astype(jnp.float32),
    )
    normal_one_mine = mine(normal_one)
    grad_inputs = grad_middle + inverse_one * (
        grad_one * mine(norm_gain) - normal_one_mine * stat_one / full_width
    )
    gain_one = jnp.sum(grad_one * normal_one_mine, axis=0)
    grad_wquery = rows_product(normed, grad_query)
    grad_wkey = rows_product(normed, grad_keys)
    grad_wvalue = rows_product(normed, grad_values)
    grad_woutgate = rows_product(normed, grad_outgate)
    grad_wrank = lax.dot_general(
        normed.astype(jnp.float32), lowrank_total, (((0,), (0,)), ((), ())), precision=PRECISE
    )
    summed = (
        lax.psum_scatter(grad_wquery, "seq", scatter_dimension=0, tiled=True),
        lax.psum_scatter(grad_wkey, "seq", scatter_dimension=0, tiled=True),
        lax.psum_scatter(grad_wvalue, "seq", scatter_dimension=0, tiled=True),
        lax.psum_scatter(grad_woutgate, "seq", scatter_dimension=0, tiled=True),
        lax.psum_scatter(grad_wrank, "seq", scatter_dimension=0, tiled=True),
        lax.psum_scatter(grad_wout, "seq", scatter_dimension=1, tiled=True),
        lax.psum_scatter(grad_wgate, "seq", scatter_dimension=0, tiled=True),
        lax.psum_scatter(grad_wup, "seq", scatter_dimension=0, tiled=True),
        lax.psum_scatter(grad_wdown, "seq", scatter_dimension=1, tiled=True),
    )
    smalls = lax.psum((grad_expand, grad_bias, gain_one, gain_two), "seq")
    return (
        output,
        grad_inputs.reshape(seq_count, span_len, part_width),
        smalls[2],
        summed[0],
        summed[1],
        summed[2],
        summed[3],
        summed[4],
        smalls[0],
        smalls[1],
        summed[5],
        smalls[3],
        summed[6],
        summed[7],
        summed[8],
    )


def solution(mesh):
    in_specs = (
        P(None, "seq", "head"),
        P(),
        P(None, "head"),
        P(None, "head"),
        P(None, "head"),
        P(None, "head"),
        P(),
        P(None, "head"),
        P("head"),
        P("head", None),
        P(),
        P(None, "head"),
        P(None, "head"),
        P("head", None),
        P(None, "seq", "head"),
    )
    out_specs = (
        P(None, "seq", "head"),
        P(None, "seq", "head"),
        P("head"),
        P("seq", "head"),
        P("seq", "head"),
        P("seq", "head"),
        P("seq", "head"),
        P("seq", None),
        P(None, "head"),
        P("head"),
        P("head", "seq"),
        P("head"),
        P("seq", "head"),
        P("seq", "head"),
        P("head", "seq"),
    )
    return jax.shard_map(body, mesh=mesh, in_specs=in_specs, out_specs=out_specs, check_vma=False)
```

profile of v0, /device:TPU:0, one launch (start us, length us, event | category | flops | bytes accessed | tf_op | source)
XLA Modules:
  0.0 891.0 jit_solution(4417193232301574513)
XLA Ops:
  7.3 7.6 all-gather
  15.0 1.0 fusion.118
  16.1 1.3 convolution_multiply_fusion
  18.9 2.3 while.84
  22.1 20.7 %all_gather.29 = f32[8,1,128]{2,1,0:T(1,128)S(1)} all-gather(f32[1,1,128]{2,1,0:T(1,128)S(1)} %slice.23), channel_id=1, replica_groups=mesh['seq'=8,'head'=4] {'seq'}, dimensions={0}, use_global_device_ids=true | all-gather | bytes 4608 | tf_op jit(solution)/shard_map/all_gather | solution.py:16
  42.8 20.7 %all-gather.7.cloned.1.call-done = f32[8,128,256]{2,1,0:T(8,128)} async-done(((f32[1,128,256]{2,1,0:T(8,128)}), f32[8,128,256]{2,1,0:T(8,128)}) %all-gather.7.cloned.1.call-update) | async-done | bytes 1048592 | tf_op jit(solution)/shard_map/all_gather | solution.py:16
  63.5 8.3 while.85
  64.6 1.0 fusion.293
  65.6 1.0 fusion.293
  66.6 1.0 fusion.293
  67.7 1.0 fusion.293
  68.7 1.0 fusion.293
  69.8 1.0 fusion.293
  70.8 1.0 fusion.293
  72.3 2.0 multiply_convert_fusion.6
  74.3 1.0 fusion.121
  75.4 5.8 all-gather.2
  81.2 14.7 %reduce-scatter.15.cloned.1.call-done = f32[128,256]{1,0:T(8,128)} async-done(((f32[128,1024]{1,0:T(8,128)}), f32[128,256]{1,0:T(8,128)}) %reduce-scatter.15.cloned.1.call-update) | async-done | bytes 131088 | tf_op jit(solution)/shard_map/reduce_scatter | solution.py:153
  96.0 1.0 fusion.95
  97.0 5.8 all_gather.32
  102.9 2.0 fusion.109
  105.6 1.2 multiply_convert_fusion.2
  107.4 1.4 convert_multiply_fusion.2
  110.9 6.1 all-reduce.1
  117.7 13.0 %reduce-scatter.19.cloned.1.call-done = f32[128,256]{1,0:T(8,128)} async-done(((f32[128,1024]{1,0:T(8,128)}), f32[128,256]{1,0:T(8,128)}) %reduce-scatter.19.cloned.1.call-update) | async-done | bytes 131088 | tf_op jit(solution)/shard_map/reduce_scatter | solution.py:182
  130.7 1.1 fusion.105
  131.8 5.8 all_gather.34
  137.5 1.5 multiply_reduce_fusion.4
  139.1 1.7 multiply_convert_fusion.5
  140.8 1.8 fusion.99
  142.7 2.4 while.82
  145.1 37.9 %all-gather.9.cloned.1.call-done = f32[1024,256]{1,0:T(8,128)} async-done(((f32[128,256]{1,0:T(8,128)}), f32[1024,256]{1,0:T(8,128)}) %all-gather.9.cloned.1.call-update) | async-done | bytes 1048592 | tf_op jit(solution)/shard_map/all_gather | solution.py:16
  183.0 8.4 while.86
  192.8 10.4 %while.83 = (s32[]{:T(128)}, f32[1,128,256]{1,2,0:T(8,128)S(1)}, f32[2,1,64,128]{3,2,1,0:T(8,128)}, bf16[2,1,64,128]{3,2,1,0:T(8,128)(2,1)}, bf16[2,1,64,256]{3,...) while((s32[]{:T(128)}, f32[1,128,256]{1,2,0:T(8,128)S(1)}, ...), condition=%wide.region_25.26_spmd.clone, body=%wide.region_20.25_spmd.sunk.clone | while | flops 146169856 | bytes 5628293 | solution.py:71
  204.1 1.4 fusion.119
  207.1 2.0 convolution_convert_fusion
  209.5 1.3 convolution_add_fusion.5
  210.8 1.2 convolution_add_fusion.7
  212.3 1.2 multiply_reduce_fusion.1
  213.6 11.6 %reduce-scatter.31.cloned.1.call-done = bf16[128,16]{0,1:T(8,128)(2,1)} async-done(((bf16[128,64]{0,1:T(8,128)(2,1)}), bf16[128,16]{0,1:T(8,128)(2,1)}) %reduce-scatter.31.cloned.1.call-update) | async-done | bytes 4112 | tf_op jit(solution)/shard_map/reduce_scatter | solution.py:236
  225.3 1.6 fusion.110
  226.9 1.3 fusion.125
  228.5 1.4 fusion.111
  229.9 1.2 fusion.114
  231.2 1.1 fusion.113
  232.4 1.4 fusion.112
  233.9 2.1 fusion.84
  236.9 2.2 fusion.107
  240.0 2.2 fusion.106
  242.4 5.3 reduce-scatter.17.cloned.1.call-done
  247.8 1.5 fusion.96
  249.3 5.7 all-reduce.2
  255.9 14.4 %reduce-scatter.21.cloned.1.call-done = bf16[128,256]{1,0:T(8,128)(2,1)} async-done(((bf16[128,1024]{1,0:T(8,128)(2,1)}), bf16[128,256]{1,0:T(8,128)(2,1)}) %reduce-scatter.21.cloned.1.call-update) | async-done | bytes 65552 | tf_op jit(solution)/shard_map/reduce_scatter | solution.py:227
  270.3 1.7 multiply_reduce_fusion.3
  272.0 37.1 %all-reduce.3 = (f32[256]{0:T(256)}, f32[16,128]{1,0:T(8,128)}, f32[128]{0:T(128)}, f32[256]{0:T(256)}) all-reduce(f32[256]{0:T(256)S(1)} %get-tuple-element.811, f32[16,128]{1,0:T(8,128)S(1)} %fusion.124, f32[128]{0:T(128)S(1)} %copy-done.58, f32[256]{0:T(256)S(1)} %get-tuple-element.809), channel_id=1, replica_groups=mesh['seq'=8,'head'=4] {'seq'}, use_global_device_ids=true, to_apply=%region_30.31 | all-reduce | flops 2688 | bytes 21504 | tf_op jit(solution)/shard_map/psum | solution.py:266
  309.1 18.9 %reduce-scatter.33.cloned.1.call-done = f32[128,16]{0,1:T(8,128)} async-done(((f32[1024,16]{0,1:T(8,128)}), f32[128,16]{0,1:T(8,128)}) %reduce-scatter.33.cloned.1.call-update) | async-done | bytes 8208 | tf_op jit(solution)/shard_map/reduce_scatter | solution.py:260
  328.0 67.2 %reduce-scatter.35.cloned.1.call-done = f32[256,128]{1,0:T(8,128)} async-done(((f32[256,1024]{1,0:T(8,128)}), f32[256,128]{1,0:T(8,128)}) %reduce-scatter.35.cloned.1.call-update) | async-done | bytes 131088 | tf_op jit(solution)/shard_map/reduce_scatter | solution.py:261
  395.3 66.3 %reduce-scatter.29.cloned.1.call-done = f32[128,256]{1,0:T(8,128)} async-done(((f32[1024,256]{1,0:T(8,128)}), f32[128,256]{1,0:T(8,128)}) %reduce-scatter.29.cloned.1.call-update) | async-done | bytes 131088 | tf_op jit(solution)/shard_map/reduce_scatter | solution.py:259
  461.5 65.3 %reduce-scatter.23.cloned.1.call-done = f32[128,128]{1,0:T(8,128)} async-done(((f32[1024,128]{1,0:T(8,128)}), f32[128,128]{1,0:T(8,128)}) %reduce-scatter.23.cloned.1.call-update) | async-done | bytes 65552 | tf_op jit(solution)/shard_map/reduce_scatter | solution.py:256
  526.9 64.8 %reduce-scatter.25.cloned.1.call-done = f32[128,128]{1,0:T(8,128)} async-done(((f32[1024,128]{1,0:T(8,128)}), f32[128,128]{1,0:T(8,128)}) %reduce-scatter.25.cloned.1.call-update) | async-done | bytes 65552 | tf_op jit(solution)/shard_map/reduce_scatter | solution.py:257
  591.6 66.7 %reduce-scatter.27.cloned.1.call-done = f32[128,256]{1,0:T(8,128)} async-done(((f32[1024,256]{1,0:T(8,128)}), f32[128,256]{1,0:T(8,128)}) %reduce-scatter.27.cloned.1.call-update) | async-done | bytes 131088 | tf_op jit(solution)/shard_map/reduce_scatter | solution.py:258
  658.3 75.4 %reduce-scatter.41.cloned.1.call-done = f32[704,128]{1,0:T(8,128)} async-done(((f32[704,1024]{1,0:T(8,128)}), f32[704,128]{1,0:T(8,128)}) %reduce-scatter.41.cloned.1.call-update) | async-done | bytes 360464 | tf_op jit(solution)/shard_map/reduce_scatter | solution.py:264
  733.8 75.4 %reduce-scatter.39.cloned.1.call-done = f32[128,704]{0,1:T(8,128)} async-done(((f32[1024,704]{0,1:T(8,128)}), f32[128,704]{0,1:T(8,128)}) %reduce-scatter.39.cloned.1.call-update) | async-done | bytes 360464 | tf_op jit(solution)/shard_map/reduce_scatter | solution.py:263
  809.1 75.4 %reduce-scatter.37.cloned.1.call-done = f32[128,704]{0,1:T(8,128)} async-done(((f32[1024,704]{0,1:T(8,128)}), f32[128,704]{0,1:T(8,128)}) %reduce-scatter.37.cloned.1.call-update) | async-done | bytes 360464 | tf_op jit(solution)/shard_map/reduce_scatter | solution.py:262
  (309 shorter events, 38.7 us)
Async XLA Ops:
  7.2 98.4 %copy-start = (bf16[704,1024]{1,0:T(8,128)(2,1)S(1)}, bf16[704,1024]{1,0:T(8,128)(2,1)}, u32[]{:S(2)}) copy-start(bf16[704,1024]{1,0:T(8,128)(2,1)} %param.38) | copy-start | bytes 4325380
  7.2 10.1 %copy-start.46 = (f32[1024]{0:T(1024)S(1)}, f32[1024]{0:T(1024)}, u32[]{:S(2)}) copy-start(f32[1024]{0:T(1024)} %param.26) | copy-start | bytes 12292
  7.2 10.1 %copy-start.43 = (bf16[1024,128]{1,0:T(8,128)(2,1)S(1)}, bf16[1024,128]{1,0:T(8,128)(2,1)}, u32[]{:S(2)}) copy-start(bf16[1024,128]{1,0:T(8,128)(2,1)} %param.28) | copy-start | bytes 786436
  7.2 10.4 %copy-start.4 = (bf16[1024,256]{1,0:T(8,128)(2,1)S(1)}, bf16[1024,256]{1,0:T(8,128)(2,1)}, u32[]{:S(2)}) copy-start(bf16[1024,256]{1,0:T(8,128)(2,1)} %param.29) | copy-start | bytes 1572868
  7.2 56.3 %all-gather.7.cloned.1.call-start = ((), (), s32[]{:S(2)}) async-start(), calls=%async_computation.28 | async-start | bytes 1179648 | tf_op jit(solution)/shard_map/all_gather | solution.py:16
  15.0 3.0 copy-start.55
  15.0 3.0 copy-start.61
  15.0 57.2 %copy-start.51 = (f32[128]{0:T(128)}, f32[128]{0:T(128)S(1)}, u32[]{:S(2)}) copy-start(f32[128]{0:T(128)S(1)} %add_rsqrt_fusion.2) | copy-start | bytes 1540
  16.1 2.8 copy-start.49
  21.8 74.1 %reduce-scatter.15.cloned.1.call-start = ((), (), s32[]{:S(2)}) async-start(), calls=%async_computation.14 | async-start | bytes 655360 | tf_op jit(solution)/shard_map/reduce_scatter | solution.py:153
  22.1 52.2 %copy-start.26 = (f32[1,128,128]{2,1,0:T(8,128)}, f32[1,128,128]{2,1,0:T(8,128)S(1)}, u32[]{:S(2)}) copy-start(f32[1,128,128]{2,1,0:T(8,128)S(1)} %reduce_window_sum.59) | copy-start | bytes 196612
  71.8 2.5 copy-start.28
  72.2 3.2 copy-start.30
  72.2 3.2 copy-start.24
  72.3 23.7 %copy-start.22 = (bf16[1,128,256]{2,1,0:T(8,128)(2,1)S(1)}, bf16[1,128,256]{2,1,0:T(8,128)(2,1)}, u32[]{:S(2)}) copy-start(bf16[1,128,256]{2,1,0:T(8,128)(2,1)} %param.25) | copy-start | bytes 196612
  74.3 30.6 %copy-start.44 = (bf16[128,256]{1,0:T(8,128)(2,1)}, bf16[128,256]{1,0:T(8,128)(2,1)S(1)}, u32[]{:S(2)}) copy-start(bf16[128,256]{1,0:T(8,128)(2,1)S(1)} %get-tuple-element.823) | copy-start | bytes 196612
  74.3 28.6 %copy-start.47 = (f32[1024]{0:T(1024)S(1)}, f32[1024]{0:T(1024)}, u32[]{:S(2)}) copy-start(f32[1024]{0:T(1024)} %param.35) | copy-start | bytes 12292
  75.4 55.3 %reduce-scatter.19.cloned.1.call-start = ((), (), s32[]{:S(2)}) async-start(), calls=%async_computation.16 | async-start | bytes 655360 | tf_op jit(solution)/shard_map/reduce_scatter | solution.py:182
  81.2 24.4 %copy-start.5 = (bf16[1,128,1024]{2,1,0:T(8,128)(2,1)}, bf16[1,128,1024]{2,1,0:T(8,128)(2,1)S(1)}, u32[]{:S(2)}) copy-start(bf16[1,128,1024]{2,1,0:T(8,128)(2,1)S(1)} %all-gather.2) | copy-start | bytes 786436
  96.0 9.0 %copy-start.3 = (bf16[1024,704]{0,1:T(8,128)(2,1)S(1)}, bf16[1024,704]{0,1:T(8,128)(2,1)}, u32[]{:S(2)}) copy-start(bf16[1024,704]{0,1:T(8,128)(2,1)} %param.37) | copy-start | bytes 4325380
  102.9 27.7 %copy-start.53 = (f32[128]{0:T(128)}, f32[128]{0:T(128)S(1)}, u32[]{:S(2)}) copy-start(f32[128]{0:T(128)S(1)} %add_rsqrt_fusion) | copy-start | bytes 1540
  106.8 1.9 copy-start.10
  106.8 1.9 copy-start.12
  107.4 30.2 %copy-start.31 = (f32[128,256]{1,0:T(8,128)S(1)}, f32[128,256]{1,0:T(8,128)}, u32[]{:S(2)}) copy-start(f32[128,256]{1,0:T(8,128)} %copy-done.30) | copy-start | bytes 393220
  108.8 74.2 %all-gather.9.cloned.1.call-start = ((), (), s32[]{:S(2)}) async-start(), calls=%async_computation.29 | async-start | bytes 1179648 | tf_op jit(solution)/shard_map/all_gather | solution.py:16
  109.0 33.7 %copy-start.56 = (f32[256]{0:T(256)}, f32[256]{0:T(256)S(1)}, u32[]{:S(2)}) copy-start(f32[256]{0:T(256)S(1)} %dynamic_slice.124) | copy-start | bytes 3076
  117.6 25.0 %copy-start.59 = (f32[128]{0:T(128)}, f32[128]{0:T(128)S(1)}, u32[]{:S(2)}) copy-start(f32[128]{0:T(128)S(1)} %fusion.101) | copy-start | bytes 1540
  137.5 5.2 copy-start.7
  142.7 82.6 %reduce-scatter.31.cloned.1.call-start = ((), (), s32[]{:S(2)}) async-start(), calls=%async_computation.22 | async-start | bytes 20480 | tf_op jit(solution)/shard_map/reduce_scatter | solution.py:236
  193.8 2.3 copy-start.35
  193.9 2.1 copy-start.41
  194.2 3.1 copy-start.39
  199.0 2.3 copy-start.35
  199.1 2.1 copy-start.41
  199.4 3.1 copy-start.39
  203.2 6.0 copy-start.38
  204.1 5.3 copy-start.33
  205.5 3.9 copy-start.17
  207.0 40.7 %reduce-scatter.17.cloned.1.call-start = ((), (), s32[]{:S(2)}) async-start(), calls=%async_computation.15 | async-start | bytes 327680 | tf_op jit(solution)/shard_map/reduce_scatter | solution.py:165
  209.1 61.2 %reduce-scatter.21.cloned.1.call-start = ((), (), s32[]{:S(2)}) async-start(), calls=%async_computation.17 | async-start | bytes 327680 | tf_op jit(solution)/shard_map/reduce_scatter | solution.py:227
  209.5 2.5 copy-start.14
  209.5 2.5 copy-start.27
  212.3 14.6 %copy-start.8 = (bf16[128,1024]{1,0:T(8,128)(2,1)S(1)}, bf16[128,1024]{1,0:T(8,128)(2,1)}, u32[]{:S(2)}) copy-start(bf16[128,1024]{1,0:T(8,128)(2,1)} %copy-done.7) | copy-start | bytes 786436
  212.3 14.6 %copy-start.45 = (bf16[128,256]{1,0:T(8,128)(2,1)S(1)}, bf16[128,256]{1,0:T(8,128)(2,1)}, u32[]{:S(2)}) copy-start(bf16[128,256]{1,0:T(8,128)(2,1)} %copy-done.44) | copy-start | bytes 196612
  213.5 14.9 %copy-start.15 = (bf16[128,256]{1,0:T(8,128)(2,1)S(1)}, bf16[128,256]{1,0:T(8,128)(2,1)}, u32[]{:S(2)}) copy-start(bf16[128,256]{1,0:T(8,128)(2,1)} %get-tuple-element.814) | copy-start | bytes 196612
  213.6 114.5 %reduce-scatter.33.cloned.1.call-start = ((), (), s32[]{:S(2)}) async-start(), calls=%async_computation.23 | async-start | bytes 73728 | tf_op jit(solution)/shard_map/reduce_scatter | solution.py:260
  226.8 168.4 %reduce-scatter.35.cloned.1.call-start = ((), (), s32[]{:S(2)}) async-start(), calls=%async_computation.24 | async-start | bytes 1179648 | tf_op jit(solution)/shard_map/reduce_scatter | solution.py:261
  228.2 233.3 %reduce-scatter.29.cloned.1.call-start = ((), (), s32[]{:S(2)}) async-start(), calls=%async_computation.21 | async-start | bytes 1179648 | tf_op jit(solution)/shard_map/reduce_scatter | solution.py:259
  229.9 2.5 copy-start.21
  229.9 297.0 %reduce-scatter.23.cloned.1.call-start = ((), (), s32[]{:S(2)}) async-start(), calls=%async_computation.18 | async-start | bytes 589824 | tf_op jit(solution)/shard_map/reduce_scatter | solution.py:256
  231.1 360.5 %reduce-scatter.25.cloned.1.call-start = ((), (), s32[]{:S(2)}) async-start(), calls=%async_computation.19 | async-start | bytes 589824 | tf_op jit(solution)/shard_map/reduce_scatter | solution.py:257
  232.4 426.0 %reduce-scatter.27.cloned.1.call-start = ((), (), s32[]{:S(2)}) async-start(), calls=%async_computation.20 | async-start | bytes 1179648 | tf_op jit(solution)/shard_map/reduce_scatter | solution.py:258
  233.8 499.9 %reduce-scatter.41.cloned.1.call-start = ((), (), s32[]{:S(2)}) async-start(), calls=%async_computation.27 | async-start | bytes 3244032 | tf_op jit(solution)/shard_map/reduce_scatter | solution.py:264
  236.0 573.1 %reduce-scatter.39.cloned.1.call-start = ((), (), s32[]{:S(2)}) async-start(), calls=%async_computation.26 | async-start | bytes 3244032 | tf_op jit(solution)/shard_map/reduce_scatter | solution.py:263
  239.1 645.4 %reduce-scatter.37.cloned.1.call-start = ((), (), s32[]{:S(2)}) async-start(), calls=%async_computation.25 | async-start | bytes 3244032 | tf_op jit(solution)/shard_map/reduce_scatter | solution.py:262
  242.3 5.5 copy-start.23
  242.3 5.5 copy-start.29
  242.3 13.4 %copy-start.18 = (f32[128,128]{1,0:T(8,128)S(1)}, f32[128,128]{1,0:T(8,128)}, u32[]{:S(2)}) copy-start(f32[128,128]{1,0:T(8,128)} %copy-done.17) | copy-start | bytes 196612
  242.3 13.5 %copy-start.50 = (f32[128,16]{0,1:T(8,128)S(1)}, f32[128,16]{0,1:T(8,128)}, u32[]{:S(2)}) copy-start(f32[128,16]{0,1:T(8,128)} %copy-done.49) | copy-start | bytes 24580
  242.3 28.0 %copy-start.25 = (bf16[1,128,256]{2,1,0:T(8,128)(2,1)S(1)}, bf16[1,128,256]{2,1,0:T(8,128)(2,1)}, u32[]{:S(2)}) copy-start(bf16[1,128,256]{2,1,0:T(8,128)(2,1)} %param.39) | copy-start | bytes 196612
  242.3 28.0 %copy-start.32 = (f32[128,256]{1,0:T(8,128)S(1)}, f32[128,256]{1,0:T(8,128)}, u32[]{:S(2)}) copy-start(f32[128,256]{1,0:T(8,128)} %reduce-scatter.19.cloned.1.call-done) | copy-start | bytes 393220
  242.3 28.0 %copy-start.57 = (f32[256]{0:T(256)S(1)}, f32[256]{0:T(256)}, u32[]{:S(2)}) copy-start(f32[256]{0:T(256)} %copy-done.56) | copy-start | bytes 3076
  242.3 28.0 %copy-start.60 = (f32[128]{0:T(128)S(1)}, f32[128]{0:T(128)}, u32[]{:S(2)}) copy-start(f32[128]{0:T(128)} %copy-done.59) | copy-start | bytes 1540
  242.3 29.7 %copy-start.58 = (f32[128]{0:T(128)S(1)}, f32[128]{0:T(128)}, u32[]{:S(2)}) copy-start(f32[128]{0:T(128)} %get-tuple-element.795) | copy-start | bytes 1540
  (23 other events, 25.1 us)
Sparse Core Ops, SparseCore 0:
  22.0 41.4 all-gather.6
  75.5 20.4 reduce-scatter.14
  108.9 21.6 reduce-scatter.18
  142.8 40.1 all-gather.8
  207.2 18.0 reduce-scatter.30
  227.7 20.0 reduce-scatter.16
  250.2 20.0 reduce-scatter.20
  274.3 53.6 reduce-scatter.32
  332.4 62.8 reduce-scatter.34
  399.1 62.4 reduce-scatter.28
  465.8 60.9 reduce-scatter.22
  530.6 60.9 reduce-scatter.24
  596.0 62.2 reduce-scatter.26
  662.3 71.3 reduce-scatter.40
  737.7 71.3 reduce-scatter.38
  813.1 71.3 reduce-scatter.36
where the time goes:
time: 892 us; the launch traced here: 891 us
  waiting for transfers between devices  693 us (78%)
  blocking collectives  94.5 us (11%)
  matrix products  44.3 us (5%)
  other arithmetic  29.2 us (3%)
  between operations  14.8 us (2%)
  local copies, waits for them, and re-layouts  13 us (1%)
    reduce_scatter x1, waiting for transfers between devices, body(): lax.psum_scatter(grad_wdown, 'seq', scatter_dimension=1, tiled=True)  75.4 us
    reduce_scatter x1, waiting for transfers between devices, body(): lax.psum_scatter(grad_wgate, 'seq', scatter_dimension=0, tiled=True)  75.4 us
    reduce_scatter x1, waiting for transfers between devices, body(): lax.psum_scatter(grad_wup, 'seq', scatter_dimension=0, tiled=True)  75.4 us
    reduce_scatter x1, waiting for transfers between devices, body(): lax.psum_scatter(grad_wout, 'seq', scatter_dimension=1, tiled=True)  67.2 us
    reduce_scatter x1, waiting for transfers between devices, body(): lax.psum_scatter(grad_wvalue, 'seq', scatter_dimension=0, tiled=True)  66.7 us
    reduce_scatter x1, waiting for transfers between devices, body(): lax.psum_scatter(grad_woutgate, 'seq', scatter_dimension=0, tiled=True)  66.3 us
    reduce_scatter x1, waiting for transfers between devices, body(): lax.psum_scatter(grad_wquery, 'seq', scatter_dimension=0, tiled=True)  65.3 us
    reduce_scatter x1, waiting for transfers between devices, body(): lax.psum_scatter(grad_wkey, 'seq', scatter_dimension=0, tiled=True)  64.8 us
  transfers between devices with their start and end apart: 16, of which 16 were waited for; matrix products, arithmetic and copies ran while one was open for 3% of the time, Pallas kernels for 0%

commit v1 on v0

--- a/solution.py
+++ b/solution.py
@@ -45,10 +45,17 @@
     )
 
 
+def running_sum(tensor):
+    length = tensor.shape[0]
+    row_index = lax.broadcasted_iota(jnp.int32, (length, length), 0)
+    col_index = lax.broadcasted_iota(jnp.int32, (length, length), 1)
+    return matmul_high((row_index >= col_index).astype(jnp.float32), tensor)
+
+
 def group_step(carry_state, block_inputs):
     q_block, k_block, v_block, g_block = block_inputs
     block_len = q_block.shape[0]
-    cumulative = jnp.cumsum(g_block, axis=0)
+    cumulative = running_sum(g_block)
     final_sum = cumulative[-1]
     q_decay = q_block * jnp.exp(cumulative)
     k_decay = k_block * jnp.exp(-cumulative)
@@ -136,7 +143,7 @@
     g_seq = per_seq(logdecay)
     zero_state = jnp.zeros((seq_count, key_width, value_width), jnp.float32)
     local_out, local_state = run_all(q_seq, k_seq, v_seq, g_seq, zero_state)
-    cumulative = jnp.cumsum(g_seq, axis=1)
+    cumulative = jax.vmap(running_sum)(g_seq)
     carry_query = q_seq * jnp.exp(cumulative)
     decay_total = cumulative[:, -1, :]
     identity = (jnp.zeros_like(decay_total), zero_state)
@@ -168,14 +175,11 @@
     output = (middle_part + ffn_mine).astype(jnp.bfloat16).reshape(seq_count, span_len, part_width)
     grad_part = cotangent.reshape(row_count, part_width)
     grad_rows = lax.all_gather(grad_part, "head", axis=1, tiled=True)
-    grad_wdown = rows_product(hidden, grad_rows)
     grad_hidden = cross_product(grad_rows, w_down)
     grad_gate = (grad_hidden * up_pre * gate_sig * (1.0 + gate_pre * (1.0 - gate_sig))).astype(
         jnp.bfloat16
     )
     grad_upper = (grad_hidden * gate_pre * gate_sig).astype(jnp.bfloat16)
-    grad_wgate = rows_product(normed_two, grad_gate)
-    grad_wup = rows_product(normed_two, grad_upper)
     grad_normed_two = cross_product(grad_gate, w_gate) + cross_product(grad_upper, w_up)
     stat_part = jnp.sum(grad_normed_two * ffn_gain * normal_two, axis=1, keepdims=True)
     grad_two, stat_two = (
@@ -190,7 +194,6 @@
     )
     gain_two = jnp.sum(grad_two * normal_mine, axis=0)
     grad_branch_rows = lax.all_gather(grad_middle.astype(jnp.bfloat16), "head", axis=1, tiled=True)
-    grad_wout = rows_product(branch, grad_branch_rows)
     grad_branch = cross_product(grad_branch_rows, w_output)
     grad_head = grad_branch * swish_gate
     grad_outgate = (
@@ -245,23 +248,36 @@
         grad_one * mine(norm_gain) - normal_one_mine * stat_one / full_width
     )
     gain_one = jnp.sum(grad_one * normal_one_mine, axis=0)
-    grad_wquery = rows_product(normed, grad_query)
-    grad_wkey = rows_product(normed, grad_keys)
-    grad_wvalue = rows_product(normed, grad_values)
-    grad_woutgate = rows_product(normed, grad_outgate)
-    grad_wrank = lax.dot_general(
-        normed.astype(jnp.float32), lowrank_total, (((0,), (0,)), ((), ())), precision=PRECISE
-    )
+    def columns_of_all(tensor):
+        return lax.all_to_all(tensor, "seq", split_axis=1, concat_axis=0, tiled=True)
+
+    def tokens_of_all(tensor):
+        return lax.all_gather(tensor, "seq", axis=0, tiled=True)
+
+    columns_one = columns_of_all(normed)
+    columns_two = columns_of_all(normed_two)
+    columns_cot = columns_of_all(grad_rows)
+    columns_branch = columns_of_all(grad_branch_rows)
+    mixer_all = tokens_of_all(
+        jnp.concatenate([grad_query, grad_keys, grad_values, grad_outgate], axis=1)
+    )
+    mixer_sum = rows_product(columns_one, mixer_all)
+    wide = key_width
+    grad_wout = rows_product(tokens_of_all(branch), columns_branch)
+    grad_wgate = rows_product(columns_two, tokens_of_all(grad_gate))
+    grad_wup = rows_product(columns_two, tokens_of_all(grad_upper))
+    grad_wdown = rows_product(tokens_of_all(hidden), columns_cot)
+    grad_wrank = rows_product(columns_one, tokens_of_all(lowrank_total.astype(jnp.bfloat16)))
     summed = (
-        lax.psum_scatter(grad_wquery, "seq", scatter_dimension=0, tiled=True),
-        lax.psum_scatter(grad_wkey, "seq", scatter_dimension=0, tiled=True),
-        lax.psum_scatter(grad_wvalue, "seq", scatter_dimension=0, tiled=True),
-        lax.psum_scatter(grad_woutgate, "seq", scatter_dimension=0, tiled=True),
-        lax.psum_scatter(grad_wrank, "seq", scatter_dimension=0, tiled=True),
-        lax.psum_scatter(grad_wout, "seq", scatter_dimension=1, tiled=True),
-        lax.psum_scatter(grad_wgate, "seq", scatter_dimension=0, tiled=True),
-        lax.psum_scatter(grad_wup, "seq", scatter_dimension=0, tiled=True),
-        lax.psum_scatter(grad_wdown, "seq", scatter_dimension=1, tiled=True),
+        mixer_sum[:, :wide],
+        mixer_sum[:, wide : 2 * wide],
+        mixer_sum[:, 2 * wide : 2 * wide + value_width],
+        mixer_sum[:, 2 * wide + value_width :],
+        grad_wrank,
+        grad_wout,
+        grad_wgate,
+        grad_wup,
+        grad_wdown,
     )
     smalls = lax.psum((grad_expand, grad_bias, gain_one, gain_two), "seq")
     return (

time: 892 us -> 452 us (0.51)
  waiting for transfers between devices: 693 us -> 175 us
  blocking collectives: 94.5 us -> 157 us
  starting transfers between devices: 0.84 us -> 14.4 us
    reduce_scatter x9 -> x0, waiting for transfers between devices: 575 us -> none  [the longest x1 75.4 us: body(): lax.psum_scatter(grad_wdown, 'seq', scatter_dimension=1, tiled=True)]
    all_gather x0 -> x2, blocking collectives: none -> 63 us  [tokens_of_all(): return lax.all_gather(tensor, 'seq', axis=0, tiled=True)]
    all_gather x0 -> x4, waiting for transfers between devices: none -> 62.4 us  [tokens_of_all(): return lax.all_gather(tensor, 'seq', axis=0, tiled=True)]
    all_to_all x0 -> x4, waiting for transfers between devices: none -> 16.4 us  [columns_of_all(): lax.all_to_all(tensor, 'seq', split_axis=1, concat_axis=0, tiled=True)]
    reduce_scatter x1, waiting for transfers between devices: 14.4 us -> 0.01 us  [body(): lax.psum_scatter(grad_normed.astype(jnp.bfloat16), 'head', scatter_dimens...]
    all_to_all x0 -> x4, starting transfers between devices: none -> 14 us  [columns_of_all(): lax.all_to_all(tensor, 'seq', split_axis=1, concat_axis=0, tiled=True)]
  transfers between devices with their start and end apart: 16 -> 15, of which waited for: 16 -> 10; matrix products, arithmetic and copies ran while one was open for 3% -> 12% of each run, Pallas kernels for 0% -> 0%
where the time goes in v1:
time: 452 us; the launch traced here: 451 us
  waiting for transfers between devices  175 us (39%)
  blocking collectives  157 us (35%)
  matrix products  42.6 us (9%)
  other arithmetic  29 us (6%)
  local copies, waits for them, and re-layouts  17 us (4%)
  between operations  14.6 us (3%)
  starting transfers between devices  14.4 us (3%)
    all_gather x2, blocking collectives, tokens_of_all(): return lax.all_gather(tensor, 'seq', axis=0, tiled=True)  63 us
    all_gather x4, waiting for transfers between devices, tokens_of_all(): return lax.all_gather(tensor, 'seq', axis=0, tiled=True)  62.4 us
    all_gather x2, waiting for transfers between devices, carried_in(): everything = jax.tree.map(lambda part: lax.all_gather(part, axis), shard)  57 us
    psum x1, blocking collectives, body(): smalls = lax.psum((grad_expand, grad_bias, gain_one, gain_two), 'seq')  35.6 us
    all_gather x1, blocking collectives, carried_in(): everything = jax.tree.map(lambda part: lax.all_gather(part, axis), shard)  20.7 us
    all_to_all x4, waiting for transfers between devices, columns_of_all(): lax.all_to_all(tensor, 'seq', split_axis=1, concat_axis=0, tiled=True)  16.4 us
    select_n x16, other arithmetic, turn(): return jax.tree.map(lambda a, b: jnp.where(reached, a, b), new, before)  16 us
    reduce_scatter x1, waiting for transfers between devices, body(): lax.psum_scatter(attn_part, 'head', scatter_dimension=1, tiled=True)  14.2 us
  transfers between devices with their start and end apart: 15, of which 10 were waited for; matrix products, arithmetic and copies ran while one was open for 12% of the time, Pallas kernels for 0%

profile of v1, /device:TPU:0, one launch (start us, length us, event | category | flops | bytes accessed | tf_op | source)
XLA Modules:
  0.0 450.6 jit_solution(3819772541969766322)
XLA Ops:
  7.3 7.6 %all-gather = bf16[1,128,1024]{2,1,0:T(8,128)(2,1)S(1)} all-gather(bf16[1,128,256]{2,1,0:T(8,128)(2,1)} %param.25), channel_id=2, replica_groups=mesh['seq'=8,'head'=4] {'head'}, dimensions={2}, use_global_device_ids=true | all-gather | bytes 327680 | tf_op jit(solution)/shard_map/all_gather | solution.py:127
  15.0 1.0 fusion.117
  16.1 1.3 fusion.116
  18.3 2.4 while.85
  21.7 20.7 %all_gather.47 = f32[8,1,128]{2,1,0:T(1,128)S(1)} all-gather(f32[1,1,128]{2,1,0:T(1,128)S(1)} %slice.43), channel_id=1, replica_groups=mesh['seq'=8,'head'=4] {'seq'}, dimensions={0}, use_global_device_ids=true | all-gather | bytes 4608 | tf_op jit(solution)/shard_map/all_gather | solution.py:16
  42.4 20.6 %all-gather.19.cloned.1.call-done = f32[8,128,256]{2,1,0:T(8,128)} async-done(((f32[1,128,256]{2,1,0:T(8,128)}), f32[8,128,256]{2,1,0:T(8,128)}) %all-gather.19.cloned.1.call-update) | async-done | bytes 1048592 | tf_op jit(solution)/shard_map/all_gather | solution.py:16
  63.0 8.3 %while.86 = (s32[]{:T(128)}, f32[1,128,256]{2,1,0:T(8,128)S(1)}, s32[]{:T(128)}, f32[8,1,128]{2,1,0:T(1,128)S(1)}, f32[8,1,128,256]{3,2,1,0:T(8,128)}) while((s32[]{:T(128)}, f32[1,128,256]{2,1,0:T(8,128)S(1)}, s32[]{:T(128)}, f32[8,1,128]{2,1,0:T(1,128)S(1)}, f32[8,1,128,256]{3,2,1,0:T(8,128)}) %tuple.267), condition=%wide.region_4.5_spmd.clone.clone, body=%wide.region_3.4_spmd.clone.sunk.clone | while | flops 131076 | bytes 394849 | solution.py:29
  63.0 1.0 fusion.317
  64.1 1.0 fusion.317
  65.1 1.0 fusion.317
  66.2 1.0 fusion.317
  67.2 1.0 fusion.317
  68.2 1.0 fusion.317
  73.4 1.0 fusion.122
  74.6 6.2 %all-gather.2 = bf16[1,128,1024]{1,2,0:T(8,128)(2,1)} all-gather(bf16[1,128,256]{1,2,0:T(8,128)(2,1)S(1)} %copy.93), channel_id=4, replica_groups=mesh['seq'=8,'head'=4] {'head'}, dimensions={2}, use_global_device_ids=true | all-gather | bytes 327680 | tf_op jit(solution)/shard_map/all_gather | solution.py:177
  80.9 14.2 %reduce-scatter.6.cloned.1.call-done = f32[128,256]{1,0:T(8,128)} async-done(((f32[128,1024]{1,0:T(8,128)}), f32[128,256]{1,0:T(8,128)}) %reduce-scatter.6.cloned.1.call-update) | async-done | bytes 131088 | tf_op jit(solution)/shard_map/reduce_scatter | solution.py:160
  95.0 1.0 fusion.98
  96.1 5.8 %all_gather.50 = bf16[128,1024]{1,0:T(8,128)(2,1)S(1)} all-gather(bf16[128,256]{1,0:T(8,128)(2,1)S(1)} %fusion.98), channel_id=1, replica_groups=mesh['seq'=8,'head'=4] {'head'}, dimensions={1}, use_global_device_ids=true | all-gather | bytes 327680 | tf_op jit(solution)/shard_map/all_gather | solution.py:162
  103.3 2.4 multiply_convert_fusion.2
  105.7 2.1 fusion.123
  107.8 2.7 convolution_add_fusion.3
  111.4 1.9 fusion.110
  113.3 6.2 %all-reduce.1 = f32[128,4]{0,1:T(4,128)S(1)} all-reduce(f32[128,4]{0,1:T(4,128)S(1)} %tile.6), channel_id=9, replica_groups=mesh['seq'=8,'head'=4] {'head'}, use_global_device_ids=true, to_apply=%region_11.12.clone | all-reduce | flops 512 | bytes 4096
  120.2 12.2 %reduce-scatter.10.cloned.1.call-done = f32[128,256]{1,0:T(8,128)} async-done(((f32[128,1024]{1,0:T(8,128)}), f32[128,256]{1,0:T(8,128)}) %reduce-scatter.10.cloned.1.call-update) | async-done | bytes 131088 | tf_op jit(solution)/shard_map/reduce_scatter | solution.py:186
  132.4 1.0 fusion.109
  133.4 5.9 %all_gather.52 = bf16[128,1024]{1,0:T(8,128)(2,1)S(1)} all-gather(bf16[128,256]{1,0:T(8,128)(2,1)S(1)} %fusion.109), channel_id=1, replica_groups=mesh['seq'=8,'head'=4] {'head'}, dimensions={1}, use_global_device_ids=true | all-gather | bytes 327680 | tf_op jit(solution)/shard_map/all_gather | solution.py:196
  139.4 1.4 multiply_reduce_fusion.4
  142.6 1.1 convolution_convert_fusion
  145.2 1.2 while.84
  146.5 36.4 %all-gather.21.cloned.1.call-done = f32[1024,256]{1,0:T(8,128)} async-done(((f32[128,256]{1,0:T(8,128)}), f32[1024,256]{1,0:T(8,128)}) %all-gather.21.cloned.1.call-update) | async-done | bytes 1048592 | tf_op jit(solution)/shard_map/all_gather | solution.py:16
  182.9 13.5 %while.87 = (s32[]{:T(128)}, f32[1,128,256]{2,1,0:T(8,128)S(1)}, s32[]{:T(128)}, f32[8,1,128]{2,1,0:T(1,128)}, f32[8,1,128,256]{3,2,1,0:T(8,128)}) while((s32[]{:T(128)}, f32[1,128,256]{2,1,0:T(8,128)S(1)}, s32[]{:T(128)}, f32[8,1,128]{2,1,0:T(1,128)}, f32[8,1,128,256]{3,2,1,0:T(8,128)}) %tuple.268), condition=%wide.region_14.15_spmd.clone.clone, body=%wide.region_13.14_spmd.clone.sunk.clone | while | flops 131080 | bytes 394895 | solution.py:29
  183.6 1.0 fusion.318
  185.3 1.0 fusion.318
  186.9 1.0 fusion.318
  188.6 1.0 fusion.318
  190.3 1.0 fusion.318
  192.0 1.0 fusion.318
  193.7 1.0 fusion.318
  195.4 1.0 fusion.318
  197.2 7.1 %while.83 = (s32[]{:T(128)}, f32[1,128,256]{1,2,0:T(8,128)S(1)}, f32[2,1,64,128]{3,2,1,0:T(8,128)S(1)}, bf16[2,1,64,128]{3,2,1,0:T(8,128)(2,1)S(1)}, bf16[2,1,64...) while((s32[]{:T(128)}, f32[1,128,256]{1,2,0:T(8,128)S(1)}, ...), condition=%wide.region_20.21_spmd.clone, body=%wide.region_17.20_spmd.sunk.clone | while | flops 157728768 | bytes 4202205 | solution.py:78
  205.8 1.4 fusion.118
  208.3 1.2 fusion.124
  211.6 2.7 multiply_reduce_fusion.1
  214.3 3.4 all-to-all-start.3
  219.2 10.3 %all-to-all-done.3 = bf16[128,8,128]{0,2,1:T(8,128)(2,1)S(1)} async-done(((bf16[128,8,128]{0,2,1:T(8,128)(2,1)}), bf16[128,8,128]{0,2,1:T(8,128)(2,1)S(1)}, u32[]{:S(2)}, u32[]{:S(2)}) %all-to-all-start.3) | async-done | bytes 262176 | tf_op jit(solution)/shard_map/all_to_all | solution.py:252
  229.6 3.6 all-to-all-start.1
  234.0 36.7 %all_gather.57 = bf16[1024,256]{1,0:T(8,128)(2,1)S(1)} all-gather(bf16[128,256]{1,0:T(8,128)(2,1)} %copy-done.27), channel_id=1, replica_groups=mesh['seq'=8,'head'=4] {'seq'}, dimensions={0}, use_global_device_ids=true | all-gather | bytes 589824 | tf_op jit(solution)/shard_map/all_gather | solution.py:255
  271.5 3.4 all-to-all-start.2
  275.0 1.5 fusion.99
  276.5 1.0 fusion.127
  277.5 6.1 %all-to-all-done.2 = bf16[128,8,128]{2,0,1:T(8,128)(2,1)S(1)} async-done(((bf16[128,8,128]{2,0,1:T(8,128)(2,1)}), bf16[128,8,128]{2,0,1:T(8,128)(2,1)S(1)}, u32[]{:S(2)}, u32[]{:S(2)}) %all-to-all-start.2) | async-done | bytes 262176 | tf_op jit(solution)/shard_map/all_to_all | solution.py:252
  283.6 2.6 fusion.130
  286.2 18.8 %all-gather.15.cloned.1.call-done = bf16[1024,704]{0,1:T(8,128)(2,1)} async-done(((bf16[128,704]{0,1:T(8,128)(2,1)}), bf16[1024,704]{0,1:T(8,128)(2,1)}) %all-gather.15.cloned.1.call-update) | async-done | bytes 1441808 | tf_op jit(solution)/shard_map/all_gather | solution.py:255
  305.0 2.6 fusion.131
  308.4 3.6 all-to-all-start
  312.0 38.9 %all-gather.17.cloned.1.call-done = bf16[1024,704]{0,1:T(8,128)(2,1)} async-done(((bf16[128,704]{0,1:T(8,128)(2,1)}), bf16[1024,704]{0,1:T(8,128)(2,1)}) %all-gather.17.cloned.1.call-update) | async-done | bytes 1441808 | tf_op jit(solution)/shard_map/all_gather | solution.py:255
  350.8 2.6 fusion.128
  353.5 5.8 %all-reduce.2 = bf16[128,4]{0,1:T(4,128)(2,1)S(1)} all-reduce(bf16[128,4]{0,1:T(4,128)(2,1)S(1)} %tile.7), channel_id=11, replica_groups=mesh['seq'=8,'head'=4] {'head'}, use_global_device_ids=true, to_apply=%region_23.24.clone | all-reduce | flops 512 | bytes 2048
  360.2 11.5 %reduce-scatter.14.cloned.1.call-done = bf16[128,16]{0,1:T(8,128)(2,1)} async-done(((bf16[128,64]{0,1:T(8,128)(2,1)}), bf16[128,16]{0,1:T(8,128)(2,1)}) %reduce-scatter.14.cloned.1.call-update) | async-done | bytes 4112 | tf_op jit(solution)/shard_map/reduce_scatter | solution.py:239
  371.7 26.3 %all_gather.56 = bf16[1024,16]{0,1:T(8,128)(2,1)S(1)} all-gather(bf16[128,16]{0,1:T(8,128)(2,1)} %reduce-scatter.14.cloned.1.call-done), channel_id=1, replica_groups=mesh['seq'=8,'head'=4] {'seq'}, dimensions={0}, use_global_device_ids=true | all-gather | bytes 36864 | tf_op jit(solution)/shard_map/all_gather | solution.py:255
  398.7 1.7 multiply_reduce_fusion.3
  400.4 35.6 %all-reduce.3 = (f32[256]{0:T(256)}, f32[16,128]{1,0:T(8,128)}, f32[128]{0:T(128)}, f32[256]{0:T(256)}) all-reduce(f32[256]{0:T(256)S(1)} %get-tuple-element.865, f32[16,128]{1,0:T(8,128)S(1)} %fusion.126, f32[128]{0:T(128)S(1)} %copy-done.47, f32[256]{0:T(256)S(1)} %get-tuple-element.863), channel_id=1, replica_groups=mesh['seq'=8,'head'=4] {'seq'}, use_global_device_ids=true, to_apply=%region_25.26 | all-reduce | flops 2688 | bytes 21504 | tf_op jit(solution)/shard_map/psum | solution.py:282
  436.0 4.8 %all-gather.11.cloned.1.call-done = bf16[1024,768]{1,0:T(8,128)(2,1)} async-done(((bf16[128,768]{1,0:T(8,128)(2,1)}), bf16[1024,768]{1,0:T(8,128)(2,1)}) %all-gather.11.cloned.1.call-update) | async-done | bytes 1572880 | tf_op jit(solution)/shard_map/all_gather | solution.py:255
  440.8 1.8 fusion.125
  (270 shorter events, 40.2 us)
Async XLA Ops:
  7.2 96.1 %copy-start = (bf16[704,1024]{1,0:T(8,128)(2,1)S(1)}, bf16[704,1024]{1,0:T(8,128)(2,1)}, u32[]{:S(2)}) copy-start(bf16[704,1024]{1,0:T(8,128)(2,1)} %param.38) | copy-start | bytes 4325380
  7.2 10.1 %copy-start.37 = (f32[1024]{0:T(1024)S(1)}, f32[1024]{0:T(1024)}, u32[]{:S(2)}) copy-start(f32[1024]{0:T(1024)} %param.26) | copy-start | bytes 12292
  7.2 10.1 %copy-start.8 = (bf16[1024,256]{1,0:T(8,128)(2,1)S(1)}, bf16[1024,256]{1,0:T(8,128)(2,1)}, u32[]{:S(2)}) copy-start(bf16[1024,256]{1,0:T(8,128)(2,1)} %param.29) | copy-start | bytes 1572868
  7.2 10.4 %copy-start.26 = (bf16[1024,128]{1,0:T(8,128)(2,1)S(1)}, bf16[1024,128]{1,0:T(8,128)(2,1)}, u32[]{:S(2)}) copy-start(bf16[1024,128]{1,0:T(8,128)(2,1)} %param.27) | copy-start | bytes 786436
  7.2 55.8 %all-gather.19.cloned.1.call-start = ((), (), s32[]{:S(2)}) async-start(), calls=%async_computation.18 | async-start | bytes 1179648 | tf_op jit(solution)/shard_map/all_gather | solution.py:16
  14.9 56.9 %copy-start.4 = (bf16[1,128,1024]{2,1,0:T(8,128)(2,1)}, bf16[1,128,1024]{2,1,0:T(8,128)(2,1)S(1)}, u32[]{:S(2)}) copy-start(bf16[1,128,1024]{2,1,0:T(8,128)(2,1)S(1)} %all-gather) | copy-start | bytes 786436
  15.0 2.9 copy-start.44
  15.0 3.0 copy-start.53
  15.0 56.7 %copy-start.42 = (f32[128]{0:T(128)}, f32[128]{0:T(128)S(1)}, u32[]{:S(2)}) copy-start(f32[128]{0:T(128)S(1)} %add_rsqrt_fusion.2) | copy-start | bytes 1540
  16.1 2.2 copy-start.40
  18.2 3.2 copy-start.35
  20.7 51.0 %copy-start.6 = (f32[2,1,64,128]{3,2,1,0:T(8,128)}, f32[2,1,64,128]{3,2,1,0:T(8,128)S(1)}, u32[]{:S(2)}) copy-start(f32[2,1,64,128]{3,2,1,0:T(8,128)S(1)} %get-tuple-element.1377) | copy-start | bytes 196612
  21.4 73.7 %reduce-scatter.6.cloned.1.call-start = ((), (), s32[]{:S(2)}) async-start(), calls=%async_computation.9 | async-start | bytes 655360 | tf_op jit(solution)/shard_map/reduce_scatter | solution.py:160
  21.4 50.3 %copy-start.19 = (bf16[1024,256]{1,0:T(8,128)(2,1)S(1)}, bf16[1024,256]{1,0:T(8,128)(2,1)}, u32[]{:S(2)}) copy-start(bf16[1024,256]{1,0:T(8,128)(2,1)} %param.30) | copy-start | bytes 1572868
  21.7 51.0 %copy-start.28 = (f32[128,128]{1,0:T(8,128)}, f32[128,128]{1,0:T(8,128)S(1)}, u32[]{:S(2)}) copy-start(f32[128,128]{1,0:T(8,128)S(1)} %fusion.102) | copy-start | bytes 196612
  71.3 1.4 copy-start.46
  71.4 2.0 copy-start.21
  72.7 1.7 copy-start.16
  72.8 22.3 %copy-start.13 = (bf16[1,128,256]{2,1,0:T(8,128)(2,1)S(1)}, bf16[1,128,256]{2,1,0:T(8,128)(2,1)}, u32[]{:S(2)}) copy-start(bf16[1,128,256]{2,1,0:T(8,128)(2,1)} %param.25) | copy-start | bytes 196612
  73.4 28.6 %copy-start.2 = (bf16[1024,704]{0,1:T(8,128)(2,1)S(1)}, bf16[1024,704]{0,1:T(8,128)(2,1)}, u32[]{:S(2)}) copy-start(bf16[1024,704]{0,1:T(8,128)(2,1)} %param.36) | copy-start | bytes 4325380
  73.4 28.6 %copy-start.36 = (f32[1024]{0:T(1024)S(1)}, f32[1024]{0:T(1024)}, u32[]{:S(2)}) copy-start(f32[1024]{0:T(1024)} %param.35) | copy-start | bytes 12292
  74.4 58.0 %reduce-scatter.10.cloned.1.call-start = ((), (), s32[]{:S(2)}) async-start(), calls=%async_computation.11 | async-start | bytes 655360 | tf_op jit(solution)/shard_map/reduce_scatter | solution.py:186
  95.0 7.6 %copy-start.3 = (bf16[1024,704]{0,1:T(8,128)(2,1)S(1)}, bf16[1024,704]{0,1:T(8,128)(2,1)}, u32[]{:S(2)}) copy-start(bf16[1024,704]{0,1:T(8,128)(2,1)} %param.37) | copy-start | bytes 4325380
  107.8 2.9 copy-start.54
  110.5 21.9 %copy-start.17 = (bf16[1,128,256]{2,1,0:T(8,128)(2,1)S(1)}, bf16[1,128,256]{2,1,0:T(8,128)(2,1)}, u32[]{:S(2)}) copy-start(bf16[1,128,256]{2,1,0:T(8,128)(2,1)} %param.39) | copy-start | bytes 196612
  110.5 28.8 %copy-start.24 = (f32[128,256]{1,0:T(8,128)S(1)}, f32[128,256]{1,0:T(8,128)}, u32[]{:S(2)}) copy-start(f32[128,256]{1,0:T(8,128)} %copy-done.23) | copy-start | bytes 393220
  110.5 28.8 %copy-start.34 = (f32[128,256]{1,0:T(8,128)S(1)}, f32[128,256]{1,0:T(8,128)}, u32[]{:S(2)}) copy-start(f32[128,256]{1,0:T(8,128)} %get-tuple-element.884) | copy-start | bytes 393220
  110.5 28.8 %copy-start.51 = (f32[128]{0:T(128)S(1)}, f32[128]{0:T(128)}, u32[]{:S(2)}) copy-start(f32[128]{0:T(128)} %copy-done.50) | copy-start | bytes 1540
  110.6 72.3 %all-gather.21.cloned.1.call-start = ((), (), s32[]{:S(2)}) async-start(), calls=%async_computation.19 | async-start | bytes 1179648 | tf_op jit(solution)/shard_map/all_gather | solution.py:16
  110.7 30.1 %copy-start.38 = (f32[256]{0:T(256)}, f32[256]{0:T(256)S(1)}, u32[]{:S(2)}) copy-start(f32[256]{0:T(256)S(1)} %dynamic_slice.124) | copy-start | bytes 3076
  113.3 28.3 %copy-start.29 = (f32[128,128]{1,0:T(8,128)S(1)}, f32[128,128]{1,0:T(8,128)}, u32[]{:S(2)}) copy-start(f32[128,128]{1,0:T(8,128)} %copy-done.28) | copy-start | bytes 196612
  120.2 20.6 %copy-start.48 = (f32[128]{0:T(128)}, f32[128]{0:T(128)S(1)}, u32[]{:S(2)}) copy-start(f32[128]{0:T(128)S(1)} %fusion.105) | copy-start | bytes 1540
  133.4 9.2 %copy-start.12 = (bf16[128,704]{0,1:T(8,128)(2,1)S(1)}, bf16[128,704]{0,1:T(8,128)(2,1)}, u32[]{:S(2)}) copy-start(bf16[128,704]{0,1:T(8,128)(2,1)} %get-tuple-element.862) | copy-start | bytes 540676
  142.5 2.6 copy-start.7
  142.6 132.4 %reduce-scatter.8.cloned.1.call-start = ((), (), s32[]{:S(2)}) async-start(), calls=%async_computation.10 | async-start | bytes 327680 | tf_op jit(solution)/shard_map/reduce_scatter | solution.py:172
  143.8 139.8 %all-gather.13.cloned.1.call-start = ((), (), s32[]{:S(2)}) async-start(), calls=%async_computation.15 | async-start | bytes 1622016 | tf_op jit(solution)/shard_map/all_gather | solution.py:255
  144.3 160.7 %all-gather.15.cloned.1.call-start = ((), (), s32[]{:S(2)}) async-start(), calls=%async_computation.16 | async-start | bytes 1622016 | tf_op jit(solution)/shard_map/all_gather | solution.py:255
  145.1 205.7 %all-gather.17.cloned.1.call-start = ((), (), s32[]{:S(2)}) async-start(), calls=%async_computation.17 | async-start | bytes 1622016 | tf_op jit(solution)/shard_map/all_gather | solution.py:255
  146.4 225.2 %reduce-scatter.14.cloned.1.call-start = ((), (), s32[]{:S(2)}) async-start(), calls=%async_computation.14 | async-start | bytes 20480 | tf_op jit(solution)/shard_map/reduce_scatter | solution.py:239
  197.1 10.1 %copy-start.45 = (bf16[16,128]{1,0:T(8,128)(2,1)S(1)}, bf16[16,128]{1,0:T(8,128)(2,1)}, u32[]{:S(2)}) copy-start(bf16[16,128]{1,0:T(8,128)(2,1)} %param.32) | copy-start | bytes 12292
  197.3 2.6 copy-start.31
  200.9 2.6 copy-start.31
  204.9 4.5 %copy-start.33 = (bf16[1024,128]{1,0:T(8,128)(2,1)S(1)}, bf16[1024,128]{1,0:T(8,128)(2,1)}, u32[]{:S(2)}) copy-start(bf16[1024,128]{1,0:T(8,128)(2,1)} %param.28) | copy-start | bytes 786436
  204.9 4.8 %copy-start.9 = (bf16[1024,256]{1,0:T(8,128)(2,1)S(1)}, bf16[1024,256]{1,0:T(8,128)(2,1)}, u32[]{:S(2)}) copy-start(bf16[1024,256]{1,0:T(8,128)(2,1)} %param.29) | copy-start | bytes 1572868
  209.5 1.1 copy-start.20
  209.7 1.8 copy-start.5
  211.5 187.2 %reduce-scatter.12.cloned.1.call-start = ((), (), s32[]{:S(2)}) async-start(), calls=%async_computation.12 | async-start | bytes 327680 | tf_op jit(solution)/shard_map/reduce_scatter | solution.py:230
  214.3 15.3 %all-to-all-start.3 = ((bf16[128,8,128]{0,2,1:T(8,128)(2,1)}), bf16[128,8,128]{0,2,1:T(8,128)(2,1)S(1)}, u32[]{:S(2)}, u32[]{:S(2)}) async-start(bf16[128,8,128]{0,2,1:T(8,128)(2,1)} %bitcast.90), calls=%async_computation.8 | async-start | bytes 524288 | tf_op jit(solution)/shard_map/all_to_all | solution.py:252
  217.7 53.0 %copy-start.10 = (bf16[16,8,8,128]{3,2,1,0:T(8,128)(2,1)S(1)}, bf16[16,8,8,128]{3,2,1,0:T(8,128)(2,1)}, u32[]{:S(2)}) copy-start(bf16[16,8,8,128]{3,2,1,0:T(8,128)(2,1)} %get-tuple-element.874) | copy-start | bytes 786436
  217.7 223.1 %all-gather.11.cloned.1.call-start = ((), (), s32[]{:S(2)}) async-start(), calls=%async_computation.13 | async-start | bytes 1769472 | tf_op jit(solution)/shard_map/all_gather | solution.py:255
  219.2 55.7 %copy-start.14 = (bf16[1,128,256]{2,1,0:T(8,128)(2,1)S(1)}, bf16[1,128,256]{2,1,0:T(8,128)(2,1)}, u32[]{:S(2)}) copy-start(bf16[1,128,256]{2,1,0:T(8,128)(2,1)} %param.25) | copy-start | bytes 196612
  219.2 55.7 %copy-start.22 = (f32[128,256]{1,0:T(8,128)S(1)}, f32[128,256]{1,0:T(8,128)}, u32[]{:S(2)}) copy-start(f32[128,256]{1,0:T(8,128)} %reduce-scatter.6.cloned.1.call-done) | copy-start | bytes 393220
  229.6 41.9 %all-to-all-start.1 = ((bf16[128,8,128]{2,0,1:T(8,128)(2,1)}), bf16[128,8,128]{2,0,1:T(8,128)(2,1)S(1)}, u32[]{:S(2)}, u32[]{:S(2)}) async-start(bf16[128,8,128]{2,0,1:T(8,128)(2,1)} %copy_bitcast_fusion.1), calls=%async_computation.6 | async-start | bytes 524288 | tf_op jit(solution)/shard_map/all_to_all | solution.py:252
  271.5 12.1 %all-to-all-start.2 = ((bf16[128,8,128]{2,0,1:T(8,128)(2,1)}), bf16[128,8,128]{2,0,1:T(8,128)(2,1)S(1)}, u32[]{:S(2)}, u32[]{:S(2)}) async-start(bf16[128,8,128]{2,0,1:T(8,128)(2,1)} %bitcast.659), calls=%async_computation.7 | async-start | bytes 524288 | tf_op jit(solution)/shard_map/all_to_all | solution.py:252
  286.2 64.6 %copy-start.11 = (bf16[8,128,128]{2,1,0:T(8,128)(2,1)S(1)}, bf16[8,128,128]{2,1,0:T(8,128)(2,1)}, u32[]{:S(2)}) copy-start(bf16[8,128,128]{2,1,0:T(8,128)(2,1)} %copy.108) | copy-start | bytes 786436
  307.6 45.8 %copy-start.52 = (bf16[128]{0:T(256)(128)(2,1)S(1)}, bf16[128]{0:T(256)(128)(2,1)}, u32[]{:S(2)}) copy-start(bf16[128]{0:T(256)(128)(2,1)} %get-tuple-element.866) | copy-start | bytes 772
  307.6 52.4 %copy-start.41 = (f32[128,16]{0,1:T(8,128)S(1)}, f32[128,16]{0,1:T(8,128)}, u32[]{:S(2)}) copy-start(f32[128,16]{0,1:T(8,128)} %copy-done.40) | copy-start | bytes 24580
  308.4 90.3 %copy-start.18 = (bf16[1,128,256]{2,1,0:T(8,128)(2,1)S(1)}, bf16[1,128,256]{2,1,0:T(8,128)(2,1)}, u32[]{:S(2)}) copy-start(bf16[1,128,256]{2,1,0:T(8,128)(2,1)} %param.39) | copy-start | bytes 196612
  308.4 90.3 %copy-start.25 = (f32[128,256]{1,0:T(8,128)S(1)}, f32[128,256]{1,0:T(8,128)}, u32[]{:S(2)}) copy-start(f32[128,256]{1,0:T(8,128)} %reduce-scatter.10.cloned.1.call-done) | copy-start | bytes 393220
  308.4 90.3 %copy-start.39 = (f32[256]{0:T(256)S(1)}, f32[256]{0:T(256)}, u32[]{:S(2)}) copy-start(f32[256]{0:T(256)} %copy-done.38) | copy-start | bytes 3076
  308.4 90.3 %copy-start.43 = (f32[128]{0:T(128)S(1)}, f32[128]{0:T(128)}, u32[]{:S(2)}) copy-start(f32[128]{0:T(128)} %copy-done.42) | copy-start | bytes 1540
  308.4 90.3 %copy-start.49 = (f32[128]{0:T(128)S(1)}, f32[128]{0:T(128)}, u32[]{:S(2)}) copy-start(f32[128]{0:T(128)} %copy-done.48) | copy-start | bytes 1540
  308.4 89.5 %all-to-all-start = ((bf16[128,8,128]{2,0,1:T(8,128)(2,1)}), bf16[128,8,128]{2,0,1:T(8,128)(2,1)S(1)}, u32[]{:S(2)}, u32[]{:S(2)}) async-start(bf16[128,8,128]{2,0,1:T(8,128)(2,1)} %bitcast.421), calls=%async_computation.4 | async-start | bytes 524288 | tf_op jit(solution)/shard_map/all_to_all | solution.py:252
  350.8 49.6 %copy-start.47 = (f32[128]{0:T(128)S(1)}, f32[128]{0:T(128)}, u32[]{:S(2)}) copy-start(f32[128]{0:T(128)} %get-tuple-element.844) | copy-start | bytes 1540
  (8 other events, 6.0 us)
Sparse Core Ops, SparseCore 0:
  21.5 41.4 all-gather.18
  74.6 20.4 reduce-scatter.5
  110.7 21.6 reduce-scatter.9
  142.7 40.1 all-gather.20
  185.8 18.9 reduce-scatter.7
  206.9 51.4 all-gather.12
  260.6 44.3 all-gather.14
  307.2 43.5 all-gather.16
  353.9 17.6 reduce-scatter.13
  374.0 19.9 reduce-scatter.11
  396.4 44.3 all-gather.10

commit v2 on v1

--- a/solution.py
+++ b/solution.py
@@ -1,7 +1,13 @@
+import functools
+
 import jax
 import jax.numpy as jnp
 from jax import lax
+from jax.experimental import pallas as pl
+from jax.experimental.pallas import tpu as pltpu
 from jax.sharding import PartitionSpec as P
+
+MESH = pl.DeviceIdType.MESH
 
 GROUP = 64
 
@@ -299,6 +305,412 @@
     )
 
 
+def dot_nn(a, b):
+    return lax.dot_general(a, b, (((1,), (0,)), ((), ())), preferred_element_type=jnp.float32)
+
+
+def fine(a, b, left, right):
+    return lax.dot_general(
+        a,
+        b,
+        (((left,), (right,)), ((), ())),
+        precision=PRECISE,
+        preferred_element_type=jnp.float32,
+    )
+
+
+def column_of(row):
+    size = row.shape[1]
+    r = lax.broadcasted_iota(jnp.int32, (size, size), 0)
+    c = lax.broadcasted_iota(jnp.int32, (size, size), 1)
+    return jnp.sum(jnp.where(r == c, jnp.broadcast_to(row, (size, size)), 0.0), 1, keepdims=True)
+
+
+HEAD_PHASES = 8
+SEQ_PHASES = 9
+
+
+def whole_kernel(S, H, *refs):
+    (x_ref, ng_ref, wq_ref, wk_ref, wv_ref, wog_ref, wr_ref, we_ref, gb_ref, wo_ref, fg_ref,
+     wg_ref, wu_ref, wd_ref, cot_ref) = refs[:15]
+    (out_ref, gin_ref, gng_ref, gwq_ref, gwk_ref, gwv_ref, gwog_ref, gwr_ref, gwe_ref, gbias_ref,
+     gwo_ref, gfg_ref, gwg_ref, gwu_ref, gwd_ref) = refs[15:30]
+    (xc, rs_a, rr_a, mid, rs_b, rr_b, rs_c, rr_c, st_two, gbuf, rs_d, rr_d, st_one,
+     dts, stf, stb, e_ref, g_ref, cs_a, cr_a, cs_b, cr_b, hid, ggu, act, fsm,
+     send_h, recv_h, send_s, recv_s) = refs[30:]
+    f32, bf16 = jnp.float32, jnp.bfloat16
+    s, h = lax.axis_index("seq"), lax.axis_index("head")
+    rows, pw = x_ref.shape
+    full = pw * H
+    cb = full // S
+    kw, vw = wq_ref.shape[1], wv_ref.shape[1]
+    blocks = rows // GROUP
+    scale = kw ** (-0.5)
+    pending = []
+
+    barrier = pltpu.get_barrier_semaphore()
+    for j in range(1, H):
+        pl.semaphore_signal(barrier, inc=1, device_id={"head": lax.rem(h + j, H)}, device_id_type=MESH)
+    for j in range(1, S):
+        pl.semaphore_signal(barrier, inc=1, device_id={"seq": lax.rem(s + j, S)}, device_id_type=MESH)
+    pl.semaphore_wait(barrier, H + S - 2)
+
+    def head_send(phase, source, target):
+        copies = []
+        for j in range(1, H):
+            peer = lax.rem(h + j, H)
+            copies.append(pltpu.make_async_remote_copy(
+                src_ref=source(peer), dst_ref=target(j), send_sem=send_h.at[phase, j],
+                recv_sem=recv_h.at[phase, j], device_id={"head": peer}, device_id_type=MESH))
+        for copy in copies:
+            copy.start()
+        pending.extend(copies)
+        return copies
+
+    def head_gather(phase, buf):
+        return head_send(phase, lambda peer: buf.at[h], lambda j: buf.at[h])
+
+    def head_scatter(phase, out, into):
+        return head_send(phase, lambda peer: out.at[peer], lambda j: into.at[j - 1])
+
+    def seq_send(phase, source, target):
+        copies = []
+        for j in range(1, S):
+            peer = lax.rem(s + j, S)
+            copies.append(pltpu.make_async_remote_copy(
+                src_ref=source(peer), dst_ref=target, send_sem=send_s.at[phase, j],
+                recv_sem=recv_s.at[phase, j], device_id={"seq": peer}, device_id_type=MESH))
+        for copy in copies:
+            copy.start()
+        pending.extend(copies)
+        return copies
+
+    def seq_gather(phase, buf):
+        return seq_send(phase, lambda peer: buf.at[s], buf.at[s])
+
+    def arrived(copies):
+        for copy in copies:
+            copy.wait_recv()
+
+    def state_copy(phase, buf, slot, peer):
+        return pltpu.make_async_remote_copy(
+            src_ref=buf.at[slot], dst_ref=buf.at[slot], send_sem=send_s.at[phase, peer],
+            recv_sem=recv_s.at[phase, slot], device_id={"seq": peer}, device_id_type=MESH)
+
+    def wide(parts):
+        return jnp.concatenate(parts, axis=1)
+
+    def summed(own, into):
+        total = own.astype(f32)
+        for j in range(H - 1):
+            total = total + into[j].astype(f32)
+        return total
+
+    xc[h, 0] = x_ref[...]
+    xc[h, 1] = cot_ref[...]
+    arrived(head_gather(0, xc))
+    norm_gain = wide([ng_ref[p] for p in range(H)])
+    ffn_gain = wide([fg_ref[p] for p in range(H)])
+    xw = wide([xc[p, 0] for p in range(H)]).astype(f32)
+    r1 = lax.rsqrt(jnp.mean(xw * xw, axis=1, keepdims=True) + EPS)
+    n1 = xw * r1
+    normed = (n1 * norm_gain).astype(bf16)
+    cot_rows = wide([xc[p, 1] for p in range(H)])
+    k = dot_nn(normed, wk_ref[...])
+    v = dot_nn(normed, wv_ref[...])
+    lowrank = dot_nn(normed, wr_ref[...])
+    expand = we_ref[...].astype(f32)
+    preact = fine(lowrank, expand, 1, 0) + gb_ref[...]
+    logdecay = (jnp.minimum(preact, 0.0) - jnp.log1p(jnp.exp(-jnp.abs(preact)))) / 16.0
+    ri = lax.broadcasted_iota(jnp.int32, (GROUP, GROUP), 0)
+    ci = lax.broadcasted_iota(jnp.int32, (GROUP, GROUP), 1)
+    lower = ri >= ci
+    tri = lower.astype(f32)
+    tri_up = (ri <= ci).astype(f32)
+
+    def part(t, b):
+        return t[b * GROUP : (b + 1) * GROUP]
+
+    span = range(blocks)
+    vb = [part(v, b) for b in span]
+    cum = [fine(tri, part(logdecay, b), 1, 0) for b in span]
+    last = [cum[b][GROUP - 1 : GROUP] for b in span]
+    ef = [jnp.exp(last[b]) for b in span]
+    kt = [part(k, b) * jnp.exp(last[b] - cum[b]) for b in span]
+    ut = [fine(vb[b], kt[b], 0, 0) for b in span]
+    state, total = ut[0], last[0]
+    for b in range(1, blocks):
+        state = state * ef[b] + ut[b]
+        total = total + last[b]
+    dts[s] = jnp.broadcast_to(total, (8, kw))
+    stf[s] = state.astype(bf16)
+    dt_copies = seq_gather(0, dts)
+    for p in range(1, S):
+        @pl.when(p > s)
+        def _():
+            state_copy(1, stf, s, p).start()
+
+    q = dot_nn(normed, wq_ref[...]) * scale
+    og = dot_nn(normed, wog_ref[...])
+    eb = [jnp.exp(cum[b]) for b in span]
+    en = [jnp.exp(-cum[b]) for b in span]
+    qd = [part(q, b) * eb[b] for b in span]
+    kd = [part(k, b) * en[b] for b in span]
+    sc = [jnp.where(lower, fine(qd[b], kd[b], 1, 1), 0.0) for b in span]
+    local = [fine(sc[b], vb[b], 1, 0) for b in span]
+    for p in range(S):
+        cs_a[p] = wide([normed[:, p * cb : (p + 1) * cb], cot_rows[:, p * cb : (p + 1) * cb]])
+    cr_a[s] = cs_a[s]
+    grad_hidden = cross_product(cot_rows, wd_ref[...])
+    osig = jax.nn.sigmoid(og)
+    swish = og * osig
+    arrived(dt_copies)
+    e_ref[...] = jnp.zeros_like(e_ref)
+    for p in range(S - 1):
+        @pl.when(p < s)
+        def _():
+            state_copy(1, stf, p, p).wait_recv()
+            e_ref[...] = e_ref[...] * jnp.exp(dts[p, 0:1]) + stf[p].astype(f32)
+    col_a = seq_send(2, lambda peer: cs_a.at[peer], cr_a.at[s])
+    et = [e_ref[...]]
+    for b in range(blocks - 1):
+        et.append(et[b] * ef[b] + ut[b])
+    mixed = jnp.concatenate([fine(qd[b], et[b], 1, 1) + local[b] for b in span], axis=0)
+    rh = lax.rsqrt(jnp.mean(mixed * mixed, axis=1, keepdims=True) + HEAD_EPS)
+    hn = mixed * rh
+    branch = (hn * swish).astype(bf16)
+    attn = dot_nn(branch, wo_ref[...])
+    for p in range(H):
+        rs_a[p] = attn[:, p * pw : (p + 1) * pw].astype(bf16)
+    arrived(head_scatter(1, rs_a, rr_a))
+    middle = x_ref[...].astype(f32) + summed(rs_a[h], rr_a)
+    mid[h] = middle.astype(bf16)
+    arrived(head_gather(2, mid))
+    mw = wide([mid[p] for p in range(H)]).astype(f32)
+    r2 = lax.rsqrt(jnp.mean(mw * mw, axis=1, keepdims=True) + EPS)
+    n2 = mw * r2
+    normed_two = (n2 * ffn_gain).astype(bf16)
+    gate = dot_nn(normed_two, wg_ref[...])
+    up = dot_nn(normed_two, wu_ref[...])
+    gsig = jax.nn.sigmoid(gate)
+    hidden = (gate * gsig * up).astype(bf16)
+    grad_gate = (grad_hidden * up * gsig * (1.0 + gate * (1.0 - gsig))).astype(bf16)
+    grad_up = (grad_hidden * gate * gsig).astype(bf16)
+    gn2 = cross_product(grad_gate, wg_ref[...]) + cross_product(grad_up, wu_ref[...])
+    ones = jnp.ones((8, full), f32)
+    st_two[h] = fine(ones, gn2 * ffn_gain * n2, 1, 1)
+    for p in range(H):
+        rs_c[p] = gn2[:, p * pw : (p + 1) * pw].astype(bf16)
+    c4 = head_scatter(3, rs_c, rr_c)
+    c5 = head_gather(4, st_two)
+    hid[s] = hidden
+    ggu[s, 0] = grad_gate
+    ggu[s, 1] = grad_up
+    ffn = dot_nn(hidden, wd_ref[...])
+    for p in range(H):
+        rs_b[p] = ffn[:, p * pw : (p + 1) * pw].astype(bf16)
+    arrived(c4)
+    arrived(c5)
+    grad_two = summed(rs_c[h], rr_c)
+    stat = st_two[0]
+    for p in range(1, H):
+        stat = stat + st_two[p]
+    n2_mine = mid[h].astype(f32) * r2
+    grad_middle = cot_ref[...].astype(f32) + r2 * (
+        grad_two * fg_ref[h] - n2_mine * (column_of(stat[0:1]) / full))
+    gain_two = jnp.sum(grad_two * n2_mine, axis=0, keepdims=True)
+    gbuf[h] = grad_middle.astype(bf16)
+    c6 = head_gather(5, gbuf)
+    c3 = head_scatter(6, rs_b, rr_b)
+    arrived(c6)
+    gbr = wide([gbuf[p] for p in range(H)])
+    gbranch = cross_product(gbr, wo_ref[...])
+    ghead = gbranch * swish
+    gog = (gbranch * hn * osig * (1.0 + og * (1.0 - osig))).astype(bf16)
+    gmix = rh * (ghead - hn * jnp.mean(ghead * hn, axis=1, keepdims=True))
+    db = [part(gmix, b) for b in span]
+    dtr = [fine(db[b], qd[b], 0, 0) for b in span]
+    pull = dtr[blocks - 1]
+    for b in reversed(range(blocks - 1)):
+        pull = pull * ef[b] + dtr[b]
+    stb[s] = pull.astype(bf16)
+    for p in range(S - 1):
+        @pl.when(p < s)
+        def _():
+            state_copy(3, stb, s, p).start()
+    arrived(c3)
+    out_ref[...] = (middle + summed(rs_b[h], rr_b)).astype(bf16)
+    for p in range(S):
+        cs_b[p] = wide([normed_two[:, p * cb : (p + 1) * cb], gbr[:, p * cb : (p + 1) * cb]])
+    cr_b[s] = cs_b[s]
+    pb = [jnp.where(lower, fine(db[b], vb[b], 1, 1), 0.0) for b in span]
+    gqd = [fine(db[b], et[b], 1, 0) + fine(pb[b], kd[b], 1, 0) for b in span]
+    gkd = [fine(pb[b], qd[b], 0, 0) for b in span]
+    gv = [fine(sc[b], db[b], 0, 0) for b in span]
+    g_ref[...] = jnp.zeros_like(g_ref)
+    for p in reversed(range(1, S)):
+        @pl.when(p > s)
+        def _():
+            state_copy(3, stb, p, p).wait_recv()
+            g_ref[...] = g_ref[...] * jnp.exp(dts[p, 0:1]) + stb[p].astype(f32)
+    hid_copies = seq_gather(4, hid)
+    ggu_copies = seq_gather(5, ggu)
+    col_b = seq_send(6, lambda peer: cs_b.at[peer], cr_b.at[s])
+    gt = [None] * blocks
+    gt[blocks - 1] = g_ref[...]
+    for b in reversed(range(1, blocks)):
+        gt[b - 1] = gt[b] * ef[b] + dtr[b]
+    gkt = [fine(vb[b], gt[b], 1, 0) for b in span]
+    gv = [gv[b] + fine(kt[b], gt[b], 1, 1) for b in span]
+    tail = [kt[b] * gkt[b] for b in span]
+    glog = [
+        fine(tri_up, qd[b] * gqd[b] - kd[b] * gkd[b] - tail[b], 1, 0)
+        + jnp.sum(tail[b], axis=0, keepdims=True)
+        + ef[b] * jnp.sum(et[b] * gt[b], axis=0, keepdims=True)
+        for b in span
+    ]
+    tall = lambda parts: jnp.concatenate(parts, axis=0)
+    grad_query = (tall([gqd[b] * eb[b] for b in span]) * scale).astype(bf16)
+    grad_keys = tall(
+        [gkd[b] * en[b] + gkt[b] * jnp.exp(last[b] - cum[b]) for b in span]).astype(bf16)
+    grad_values = tall(gv).astype(bf16)
+    act[s] = wide([branch, grad_query, grad_keys, grad_values, gog])
+    act_copies = seq_gather(7, act)
+    grad_pre = tall(glog) / 16.0 * jax.nn.sigmoid(-preact)
+    grad_expand = fine(lowrank, grad_pre, 0, 0)
+    grad_bias = jnp.sum(grad_pre, axis=0, keepdims=True)
+    glow = fine(grad_pre, expand, 1, 1)
+    glow_t = fine(expand, grad_pre, 1, 1)
+    gnormed = (
+        cross_product(grad_query, wq_ref[...])
+        + cross_product(grad_keys, wk_ref[...])
+        + cross_product(grad_values, wv_ref[...])
+        + cross_product(gog, wog_ref[...])
+        + fine(glow, wr_ref[...].astype(f32), 1, 1)
+    )
+    rank = glow_t.shape[0]
+    st_one[h, 0:8] = fine(ones, gnormed * norm_gain * n1, 1, 1)
+    st_one[h, 8 : 8 + rank] = glow_t
+    for p in range(H):
+        rs_d[p] = gnormed[:, p * pw : (p + 1) * pw].astype(bf16)
+    c7 = head_scatter(7, rs_d, rr_d)
+    c8 = head_gather(8, st_one)
+    arrived(c7)
+    arrived(c8)
+    grad_one = summed(rs_d[h], rr_d)
+    small = st_one[0]
+    for p in range(1, H):
+        small = small + st_one[p]
+    n1_mine = x_ref[...].astype(f32) * r1
+    gin_ref[...] = grad_middle + r1 * (
+        grad_one * ng_ref[h] - n1_mine * (column_of(small[0:1]) / full))
+    gain_one = jnp.sum(grad_one * n1_mine, axis=0, keepdims=True)
+    lanes = rows
+    chunks = [grad_bias]
+    for gain in (gain_one, gain_two):
+        chunks += [gain[:, i * lanes : (i + 1) * lanes] for i in range(pw // lanes)]
+    used = len(chunks)
+    chunks.append(jnp.zeros((8 - used, lanes), f32))
+    fsm[s, 0:rank] = grad_expand
+    fsm[s, rank : rank + 8] = tall(chunks)
+    fsm[s, rank + 8 : 2 * rank + 8] = small[8 : 8 + rank]
+    fsm_copies = seq_gather(8, fsm)
+
+    def tokens(t):
+        return t.reshape(S * rows, t.shape[-1])
+
+    arrived(col_a)
+    cols_one = tokens(cr_a[...])
+    arrived(hid_copies)
+    gwd_ref[...] = rows_product(tokens(hid[...]), cols_one[:, cb:])
+    arrived(ggu_copies)
+    arrived(col_b)
+    cols_two = tokens(cr_b[...])
+    gwg_ref[...] = rows_product(cols_two[:, :cb], tokens(ggu[:, 0]))
+    gwu_ref[...] = rows_product(cols_two[:, :cb], tokens(ggu[:, 1]))
+    arrived(act_copies)
+    gwo_ref[...] = rows_product(tokens(act[:, :, :vw]), tokens(cr_b[:, :, cb:]))
+    mixes = rows_product(tokens(cr_a[:, :, :cb]), tokens(act[:, :, vw:]))
+    gwq_ref[...] = mixes[:, :kw]
+    gwk_ref[...] = mixes[:, kw : 2 * kw]
+    gwv_ref[...] = mixes[:, 2 * kw : 2 * kw + vw]
+    gwog_ref[...] = mixes[:, 2 * kw + vw :]
+    arrived(fsm_copies)
+    smalls = fsm[0]
+    for p in range(1, S):
+        smalls = smalls + fsm[p]
+    gwe_ref[...] = smalls[:rank]
+    gbias_ref[...] = smalls[rank : rank + 1]
+    half = pw // lanes
+    gng_ref[...] = wide([smalls[rank + 1 + i : rank + 2 + i] for i in range(half)])
+    gfg_ref[...] = wide([smalls[rank + 1 + half + i : rank + 2 + half + i] for i in range(half)])
+    acc = jnp.zeros((rank, cb), f32)
+    for p in range(S):
+        acc = acc + fine(fsm[p, rank + 8 : 2 * rank + 8], cr_a[p, :, :cb].astype(f32), 1, 0)
+    gwr_ref[...] = acc
+    for copy in pending:
+        copy.wait_send()
+    for p in range(S):
+        @pl.when(p > s)
+        def _():
+            state_copy(1, stf, s, p).wait_send()
+
+        @pl.when(p < s)
+        def _():
+            state_copy(3, stb, s, p).wait_send()
+
+
+def kernel_body(block_input, norm_gain, w_query, w_key, w_value, w_outgate, w_rank, w_expand,
+                gate_bias, w_output, ffn_gain, w_gate, w_up, w_down, cotangent):
+    S, H = lax.axis_size("seq"), lax.axis_size("head")
+    rows, pw = block_input.shape[1:]
+    full = pw * H
+    cb = full // S
+    kw, vw, rank, ff = w_query.shape[1], w_value.shape[1], w_rank.shape[1], w_gate.shape[1]
+    f32, bf16 = jnp.float32, jnp.bfloat16
+
+    def shape(dims, dtype=f32):
+        return jax.ShapeDtypeStruct(dims, dtype)
+
+    outs = [shape((rows, pw), bf16), shape((rows, pw)), shape((1, pw)), shape((cb, kw)), shape((cb, kw)),
+            shape((cb, vw)), shape((cb, vw)), shape((rank, cb)), shape((rank, kw)), shape((1, kw)),
+            shape((vw, cb)), shape((1, pw)), shape((cb, ff)), shape((cb, ff)), shape((ff, cb))]
+
+    def own(*dims, dtype=bf16):
+        return pltpu.VMEM(dims, dtype)
+
+    scratch = [
+        own(H, 2, rows, pw), own(H, rows, pw), own(H - 1, rows, pw), own(H, rows, pw),
+        own(H, rows, pw), own(H - 1, rows, pw), own(H, rows, pw), own(H - 1, rows, pw),
+        own(H, 8, rows, dtype=f32), own(H, rows, pw), own(H, rows, pw), own(H - 1, rows, pw),
+        own(H, 8 + rank, rows, dtype=f32), own(S, 8, kw, dtype=f32), own(S, vw, kw),
+        own(S, vw, kw), own(vw, kw, dtype=f32), own(vw, kw, dtype=f32),
+        own(S, rows, 2 * cb), own(S, rows, 2 * cb), own(S, rows, 2 * cb), own(S, rows, 2 * cb),
+        own(S, rows, ff), own(S, 2, rows, ff), own(S, rows, 2 * kw + 3 * vw),
+        own(S, 2 * rank + 8, rows, dtype=f32),
+        pltpu.SemaphoreType.DMA((HEAD_PHASES + 1, H)), pltpu.SemaphoreType.DMA((HEAD_PHASES + 1, H)),
+        pltpu.SemaphoreType.DMA((SEQ_PHASES, S)), pltpu.SemaphoreType.DMA((SEQ_PHASES, S)),
+    ]
+    got = pl.pallas_call(
+        functools.partial(whole_kernel, S, H),
+        out_shape=outs,
+        in_specs=[pl.BlockSpec(memory_space=pltpu.VMEM)] * 15,
+        out_specs=[pl.BlockSpec(memory_space=pltpu.VMEM)] * 15,
+        scratch_shapes=scratch,
+        compiler_params=pltpu.CompilerParams(
+            collective_id=0, has_side_effects=True, vmem_limit_bytes=56 * 1024 * 1024),
+    )(block_input.reshape(rows, pw), norm_gain.reshape(H, 1, pw), w_query, w_key, w_value, w_outgate,
+      w_rank, w_expand, gate_bias.reshape(1, kw), w_output, ffn_gain.reshape(H, 1, pw), w_gate, w_up,
+      w_down, cotangent.reshape(rows, pw))
+    got = list(got)
+    got[0] = got[0].reshape(1, rows, pw)
+    got[1] = got[1].reshape(1, rows, pw)
+    for i in (2, 9, 11):
+        got[i] = got[i].reshape(-1)
+    got[7] = got[7].T
+    return tuple(got)
+
+
 def solution(mesh):
     in_specs = (
         P(None, "seq", "head"),
@@ -334,4 +746,5 @@
         P("seq", "head"),
         P("head", "seq"),
     )
-    return jax.shard_map(body, mesh=mesh, in_specs=in_specs, out_specs=out_specs, check_vma=False)
+    part = kernel_body if mesh.shape["seq"] <= 8 else body
+    return jax.shard_map(part, mesh=mesh, in_specs=in_specs, out_specs=out_specs, check_vma=False)

time: 452 us -> 249 us (0.55)
  Pallas kernels: 0 us -> 230 us
  waiting for transfers between devices: 175 us -> 0 us
  blocking collectives: 157 us -> 0 us
  matrix products: 42.6 us -> 0 us
  other arithmetic: 29 us -> 0 us
  starting transfers between devices: 14.4 us -> 0 us
  between operations: 14.6 us -> 0.77 us
    pallas_call x0 -> x1, Pallas kernels: none -> 230 us  [kernel_body(): pl.pallas_call(functools.partial(whole_kernel, S, H), out_shape=outs, in_...]
    all_gather x6 -> x0, waiting for transfers between devices: 119 us -> none  [the longest x4 62.4 us: tokens_of_all(): return lax.all_gather(tensor, 'seq', axis=0, tiled=True)]
    all_gather x7 -> x0, blocking collectives: 109 us -> none  [the longest x2 63 us: tokens_of_all(): return lax.all_gather(tensor, 'seq', axis=0, tiled=True)]
    dot_general x66 -> x0, matrix products: 42.6 us -> none  [the longest x6 11.5 us: rows_product(): lax.dot_general(left_side, right_side, (((0,), (0,)), ((), ())), preferre...]
    reduce_scatter x5 -> x0, waiting for transfers between devices: 37.9 us -> none  [the longest x1 14.2 us: body(): lax.psum_scatter(attn_part, 'head', scatter_dimension=1, tiled=True)]
    psum x1 -> x0, blocking collectives: 35.6 us -> none  [body(): smalls = lax.psum((grad_expand, grad_bias, gain_one, gain_two), 'seq')]
    all_to_all x4 -> x0, waiting for transfers between devices: 16.4 us -> none  [columns_of_all(): lax.all_to_all(tensor, 'seq', split_axis=1, concat_axis=0, tiled=True)]
    select_n x16 -> x0, other arithmetic: 16 us -> none  [turn(): return jax.tree.map(lambda a, b: jnp.where(reached, a, b), new, before)]
  transfers between devices with their start and end apart: 15 -> 0, of which waited for: 10 -> 0; matrix products, arithmetic and copies ran while one was open for 12% -> 0% of each run, Pallas kernels for 0% -> 0%
where the time goes in v2:
time: 249 us; the launch traced here: 248 us
  Pallas kernels  230 us (92%)
  local copies, waits for them, and re-layouts  18 us (7%)
    pallas_call x1, Pallas kernels, kernel_body(): pl.pallas_call(functools.partial(whole_kernel, S, H), out_shape=outs, in_...  230 us
    unnamed x46, local copies, waits for them, and re-layouts  18 us

profile of v2, /device:TPU:0, one launch (start us, length us, event | category | flops | bytes accessed | tf_op | source)
XLA Modules:
  0.0 248.3 jit_solution(1362257904943778315)
XLA Ops:
  0.6 1.6 copy.30.refs_6_
  2.2 0.0 copy-start
  2.2 2.7 %copy.31.refs_11_ = bf16[1024,704]{1,0:T(8,128)(2,1)} copy(bf16[1024,704]{0,1:T(8,128)(2,1)} %param.26) | data formatting | bytes 2883584 | tf_op args[11]
  5.0 0.0 copy-done
  5.0 1.6 copy.32.refs_12_
  6.5 229.5 %shard_map.262 = (bf16[128,256]{1,0:T(8,128)(2,1)}, f32[128,256]{1,0:T(8,128)}, f32[1,256]{1,0:T(1,128)}, f32[128,128]{1,0:T(8,128)}, f32[128,128]{1,0:T(8,128)}...) custom-call(bf16[128,256]{1,0:T(8,128)(2,1)} %bitcast.13, ...), custom_call_target="tpu_custom_call" | custom-call | tf_op jit(solution)/shard_map/pallas_call | solution.py:694
  236.0 0.0 copy-start.8
  236.1 0.0 copy-start.5
  236.1 0.0 copy-start.12
  236.1 0.0 copy-start.7
  236.1 0.0 copy-start.6
  236.1 0.0 copy-start.4
  236.1 0.0 copy-start.3
  236.1 0.0 copy-start.10
  236.1 0.0 copy-start.9
  236.1 0.0 copy-start.13
  236.1 0.0 copy-start.2
  236.2 0.0 copy-start.11
  236.2 0.0 copy-start.1
  236.2 2.1 copy.33
  238.3 1.9 copy.34
  240.2 0.0 copy-done.8
  240.2 0.6 copy.48
  240.8 0.0 copy-done.5
  240.8 0.7 copy.49
  241.5 0.0 copy-done.12
  241.5 0.6 copy.50
  242.0 0.0 copy-done.7
  242.0 0.6 copy.51
  242.7 0.0 copy-done.6
  242.7 0.6 copy.52
  243.3 0.0 copy-done.4
  243.3 0.7 copy.53
  244.0 0.0 copy-done.3
  244.0 0.7 copy.54
  244.6 0.0 copy-done.10
  244.6 0.6 copy.55
  245.2 0.0 copy-done.9
  245.2 0.6 copy.56
  245.8 0.0 copy-done.13
  245.8 0.5 copy.57
  246.3 0.0 copy-done.2
  246.3 0.7 copy.58
  247.0 0.0 copy-done.11
  247.0 0.6 copy.59
  247.6 0.0 copy-done.1
  247.6 0.7 copy.60
Async XLA Ops:
  2.2 2.7 %copy-start = (bf16[1024,704]{0,1:T(8,128)(2,1)S(1)}, bf16[1024,704]{0,1:T(8,128)(2,1)}, u32[]{:S(2)}) copy-start(bf16[1024,704]{0,1:T(8,128)(2,1)} %param.27) | copy-start | bytes 4325380
  236.0 4.1 %copy-start.8 = (bf16[128,256]{1,0:T(8,128)(2,1)S(1)}, bf16[128,256]{1,0:T(8,128)(2,1)}, u32[]{:S(2)}) copy-start(bf16[128,256]{1,0:T(8,128)(2,1)} %get-tuple-element.30) | copy-start | bytes 196612
  236.1 4.8 %copy-start.5 = (f32[128,256]{1,0:T(8,128)S(1)}, f32[128,256]{1,0:T(8,128)}, u32[]{:S(2)}) copy-start(f32[128,256]{1,0:T(8,128)} %get-tuple-element.31) | copy-start | bytes 393220
  236.1 5.4 %copy-start.12 = (f32[1,256]{1,0:T(1,128)S(1)}, f32[1,256]{1,0:T(1,128)}, u32[]{:S(2)}) copy-start(f32[1,256]{1,0:T(1,128)} %get-tuple-element.32) | copy-start | bytes 3076
  236.1 6.0 %copy-start.7 = (f32[128,128]{1,0:T(8,128)S(1)}, f32[128,128]{1,0:T(8,128)}, u32[]{:S(2)}) copy-start(f32[128,128]{1,0:T(8,128)} %get-tuple-element.78) | copy-start | bytes 196612
  236.1 6.6 %copy-start.6 = (f32[128,128]{1,0:T(8,128)S(1)}, f32[128,128]{1,0:T(8,128)}, u32[]{:S(2)}) copy-start(f32[128,128]{1,0:T(8,128)} %get-tuple-element.79) | copy-start | bytes 196612
  236.1 7.2 %copy-start.4 = (f32[128,256]{1,0:T(8,128)S(1)}, f32[128,256]{1,0:T(8,128)}, u32[]{:S(2)}) copy-start(f32[128,256]{1,0:T(8,128)} %get-tuple-element.80) | copy-start | bytes 393220
  236.1 7.9 %copy-start.3 = (f32[128,256]{1,0:T(8,128)S(1)}, f32[128,256]{1,0:T(8,128)}, u32[]{:S(2)}) copy-start(f32[128,256]{1,0:T(8,128)} %get-tuple-element.81) | copy-start | bytes 393220
  236.1 8.5 %copy-start.10 = (f32[16,128]{1,0:T(8,128)S(1)}, f32[16,128]{1,0:T(8,128)}, u32[]{:S(2)}) copy-start(f32[16,128]{1,0:T(8,128)} %get-tuple-element.37) | copy-start | bytes 24580
  236.1 9.1 %copy-start.9 = (f32[16,128]{1,0:T(8,128)S(1)}, f32[16,128]{1,0:T(8,128)}, u32[]{:S(2)}) copy-start(f32[16,128]{1,0:T(8,128)} %get-tuple-element.83) | copy-start | bytes 24580
  236.1 9.7 %copy-start.13 = (f32[1,128]{1,0:T(1,128)S(1)}, f32[1,128]{1,0:T(1,128)}, u32[]{:S(2)}) copy-start(f32[1,128]{1,0:T(1,128)} %get-tuple-element.39) | copy-start | bytes 1540
  236.1 10.2 %copy-start.2 = (f32[256,128]{1,0:T(8,128)S(1)}, f32[256,128]{1,0:T(8,128)}, u32[]{:S(2)}) copy-start(f32[256,128]{1,0:T(8,128)} %get-tuple-element.85) | copy-start | bytes 393220
  236.2 10.8 %copy-start.11 = (f32[1,256]{1,0:T(1,128)S(1)}, f32[1,256]{1,0:T(1,128)}, u32[]{:S(2)}) copy-start(f32[1,256]{1,0:T(1,128)} %get-tuple-element.41) | copy-start | bytes 3076
  236.2 11.4 %copy-start.1 = (f32[704,128]{1,0:T(8,128)S(1)}, f32[704,128]{1,0:T(8,128)}, u32[]{:S(2)}) copy-start(f32[704,128]{1,0:T(8,128)} %get-tuple-element.89) | copy-start | bytes 1081348

commit v3 on v2

--- a/solution.py
+++ b/solution.py
@@ -396,6 +396,22 @@
         return pltpu.make_async_remote_copy(
             src_ref=buf.at[slot], dst_ref=buf.at[slot], send_sem=send_s.at[phase, peer],
             recv_sem=recv_s.at[phase, slot], device_id={"seq": peer}, device_id_type=MESH)
+
+    def flip(t, n):
+        return t + n - 2 * n * lax.rem(lax.div(t, n), 2)
+
+    def relay(n, slots, first):
+        copies = []
+        for phase, buf in ((4, hid), (5, ggu)):
+            for i, slot in enumerate(slots):
+                copies.append(pltpu.make_async_remote_copy(
+                    src_ref=buf.at[slot], dst_ref=buf.at[slot], send_sem=send_s.at[phase, first + i],
+                    recv_sem=recv_s.at[phase, first + i], device_id={"seq": flip(s, n)},
+                    device_id_type=MESH))
+        for copy in copies:
+            copy.start()
+        pending.extend(copies)
+        return copies
 
     def wide(parts):
         return jnp.concatenate(parts, axis=1)
@@ -506,6 +522,7 @@
     hid[s] = hidden
     ggu[s, 0] = grad_gate
     ggu[s, 1] = grad_up
+    relay_one = relay(4, [s], 1)
     ffn = dot_nn(hidden, wd_ref[...])
     for p in range(H):
         rs_b[p] = ffn[:, p * pw : (p + 1) * pw].astype(bf16)
@@ -538,6 +555,8 @@
         @pl.when(p < s)
         def _():
             state_copy(3, stb, s, p).start()
+    arrived(relay_one)
+    relay_two = relay(2, [s, flip(s, 4)], 2)
     arrived(c3)
     out_ref[...] = (middle + summed(rs_b[h], rr_b)).astype(bf16)
     for p in range(S):
@@ -553,8 +572,8 @@
         def _():
             state_copy(3, stb, p, p).wait_recv()
             g_ref[...] = g_ref[...] * jnp.exp(dts[p, 0:1]) + stb[p].astype(f32)
-    hid_copies = seq_gather(4, hid)
-    ggu_copies = seq_gather(5, ggu)
+    arrived(relay_two)
+    relay_three = relay(1, [s, flip(s, 4), flip(s, 2), flip(flip(s, 2), 4)], 4)
     col_b = seq_send(6, lambda peer: cs_b.at[peer], cr_b.at[s])
     gt = [None] * blocks
     gt[blocks - 1] = g_ref[...]
@@ -621,9 +640,8 @@
 
     arrived(col_a)
     cols_one = tokens(cr_a[...])
-    arrived(hid_copies)
+    arrived(relay_three)
     gwd_ref[...] = rows_product(tokens(hid[...]), cols_one[:, cb:])
-    arrived(ggu_copies)
     arrived(col_b)
     cols_two = tokens(cr_b[...])
     gwg_ref[...] = rows_product(cols_two[:, :cb], tokens(ggu[:, 0]))
@@ -746,5 +764,5 @@
         P("seq", "head"),
         P("head", "seq"),
     )
-    part = kernel_body if mesh.shape["seq"] <= 8 else body
+    part = kernel_body if mesh.shape["seq"] == 8 else body
     return jax.shard_map(part, mesh=mesh, in_specs=in_specs, out_specs=out_specs, check_vma=False)

time: 249 us -> 203 us (0.82)
  Pallas kernels: 230 us -> 184 us
    pallas_call x1, Pallas kernels: 230 us -> 184 us  [kernel_body(): pl.pallas_call(functools.partial(whole_kernel, S, H), out_shape=outs, in_...]
where the time goes in v3:
time: 203 us
  Pallas kernels  184 us (91%)
  local copies, waits for them, and re-layouts  18 us (9%)
    pallas_call x1, Pallas kernels, kernel_body(): pl.pallas_call(functools.partial(whole_kernel, S, H), out_shape=outs, in_...  184 us
    unnamed x46, local copies, waits for them, and re-layouts  18 us

profile of v3, /device:TPU:0, one launch (start us, length us, event | category | flops | bytes accessed | tf_op | source)
XLA Modules:
  0.0 203.2 jit_solution(7078767982308350474)
XLA Ops:
  0.6 1.6 copy.30.refs_6_
  2.2 0.0 copy-start
  2.2 2.7 %copy.31.refs_11_ = bf16[1024,704]{1,0:T(8,128)(2,1)} copy(bf16[1024,704]{0,1:T(8,128)(2,1)} %param.26) | data formatting | bytes 2883584 | tf_op args[11]
  5.0 0.0 copy-done
  5.0 1.6 copy.32.refs_12_
  6.5 184.4 %shard_map.262 = (bf16[128,256]{1,0:T(8,128)(2,1)}, f32[128,256]{1,0:T(8,128)}, f32[1,256]{1,0:T(1,128)}, f32[128,128]{1,0:T(8,128)}, f32[128,128]{1,0:T(8,128)}...) custom-call(bf16[128,256]{1,0:T(8,128)(2,1)} %bitcast.13, ...), custom_call_target="tpu_custom_call" | custom-call | tf_op jit(solution)/shard_map/pallas_call | solution.py:712
  191.0 0.0 copy-start.8
  191.0 0.0 copy-start.5
  191.0 0.0 copy-start.12
  191.0 0.0 copy-start.7
  191.0 0.0 copy-start.6
  191.0 0.0 copy-start.4
  191.0 0.0 copy-start.3
  191.0 0.0 copy-start.10
  191.0 0.0 copy-start.9
  191.0 0.0 copy-start.13
  191.1 0.0 copy-start.2
  191.1 0.0 copy-start.11
  191.1 0.0 copy-start.1
  191.1 2.1 %copy.33 = f32[128,704]{0,1:T(8,128)} copy(f32[128,704]{1,0:T(8,128)} %get-tuple-element.57) | data formatting | bytes 720896
  193.2 1.9 copy.34
  195.1 0.0 copy-done.8
  195.1 0.6 copy.48
  195.7 0.0 copy-done.5
  195.7 0.7 copy.49
  196.4 0.0 copy-done.12
  196.4 0.6 copy.50
  196.9 0.0 copy-done.7
  196.9 0.6 copy.51
  197.6 0.0 copy-done.6
  197.6 0.6 copy.52
  198.2 0.0 copy-done.4
  198.2 0.7 copy.53
  198.9 0.0 copy-done.3
  198.9 0.7 copy.54
  199.5 0.0 copy-done.10
  199.5 0.6 copy.55
  200.1 0.0 copy-done.9
  200.1 0.6 copy.56
  200.7 0.0 copy-done.13
  200.7 0.5 copy.57
  201.2 0.0 copy-done.2
  201.2 0.7 copy.58
  201.9 0.0 copy-done.11
  201.9 0.6 copy.59
  202.5 0.0 copy-done.1
  202.5 0.7 copy.60
Async XLA Ops:
  2.2 2.7 %copy-start = (bf16[1024,704]{0,1:T(8,128)(2,1)S(1)}, bf16[1024,704]{0,1:T(8,128)(2,1)}, u32[]{:S(2)}) copy-start(bf16[1024,704]{0,1:T(8,128)(2,1)} %param.27) | copy-start | bytes 4325380
  191.0 4.1 %copy-start.8 = (bf16[128,256]{1,0:T(8,128)(2,1)S(1)}, bf16[128,256]{1,0:T(8,128)(2,1)}, u32[]{:S(2)}) copy-start(bf16[128,256]{1,0:T(8,128)(2,1)} %get-tuple-element.30) | copy-start | bytes 196612
  191.0 4.8 %copy-start.5 = (f32[128,256]{1,0:T(8,128)S(1)}, f32[128,256]{1,0:T(8,128)}, u32[]{:S(2)}) copy-start(f32[128,256]{1,0:T(8,128)} %get-tuple-element.31) | copy-start | bytes 393220
  191.0 5.4 %copy-start.12 = (f32[1,256]{1,0:T(1,128)S(1)}, f32[1,256]{1,0:T(1,128)}, u32[]{:S(2)}) copy-start(f32[1,256]{1,0:T(1,128)} %get-tuple-element.32) | copy-start | bytes 3076
  191.0 6.0 %copy-start.7 = (f32[128,128]{1,0:T(8,128)S(1)}, f32[128,128]{1,0:T(8,128)}, u32[]{:S(2)}) copy-start(f32[128,128]{1,0:T(8,128)} %get-tuple-element.78) | copy-start | bytes 196612
  191.0 6.6 %copy-start.6 = (f32[128,128]{1,0:T(8,128)S(1)}, f32[128,128]{1,0:T(8,128)}, u32[]{:S(2)}) copy-start(f32[128,128]{1,0:T(8,128)} %get-tuple-element.79) | copy-start | bytes 196612
  191.0 7.2 %copy-start.4 = (f32[128,256]{1,0:T(8,128)S(1)}, f32[128,256]{1,0:T(8,128)}, u32[]{:S(2)}) copy-start(f32[128,256]{1,0:T(8,128)} %get-tuple-element.80) | copy-start | bytes 393220
  191.0 7.9 %copy-start.3 = (f32[128,256]{1,0:T(8,128)S(1)}, f32[128,256]{1,0:T(8,128)}, u32[]{:S(2)}) copy-start(f32[128,256]{1,0:T(8,128)} %get-tuple-element.81) | copy-start | bytes 393220
  191.0 8.5 %copy-start.10 = (f32[16,128]{1,0:T(8,128)S(1)}, f32[16,128]{1,0:T(8,128)}, u32[]{:S(2)}) copy-start(f32[16,128]{1,0:T(8,128)} %get-tuple-element.37) | copy-start | bytes 24580
  191.0 9.1 %copy-start.9 = (f32[16,128]{1,0:T(8,128)S(1)}, f32[16,128]{1,0:T(8,128)}, u32[]{:S(2)}) copy-start(f32[16,128]{1,0:T(8,128)} %get-tuple-element.83) | copy-start | bytes 24580
  191.0 9.7 %copy-start.13 = (f32[1,128]{1,0:T(1,128)S(1)}, f32[1,128]{1,0:T(1,128)}, u32[]{:S(2)}) copy-start(f32[1,128]{1,0:T(1,128)} %get-tuple-element.39) | copy-start | bytes 1540
  191.1 10.2 %copy-start.2 = (f32[256,128]{1,0:T(8,128)S(1)}, f32[256,128]{1,0:T(8,128)}, u32[]{:S(2)}) copy-start(f32[256,128]{1,0:T(8,128)} %get-tuple-element.85) | copy-start | bytes 393220
  191.1 10.8 %copy-start.11 = (f32[1,256]{1,0:T(1,128)S(1)}, f32[1,256]{1,0:T(1,128)}, u32[]{:S(2)}) copy-start(f32[1,256]{1,0:T(1,128)} %get-tuple-element.41) | copy-start | bytes 3076
  191.1 11.4 %copy-start.1 = (f32[704,128]{1,0:T(8,128)S(1)}, f32[704,128]{1,0:T(8,128)}, u32[]{:S(2)}) copy-start(f32[704,128]{1,0:T(8,128)} %get-tuple-element.89) | copy-start | bytes 1081348
